TPU v7x, 32 devices: a whole 2x2x4 slice. The times are simulated.
32 devices in a mesh: ctx: 4 (over y, x), tp: 8 (over z, core).
Axes of the slice: x: 2, y: 2, z: 4, core: 2. Of those that a mesh axis runs over, the one named last changes fastest.
Arguments:
- short_query: bfloat16 [4096, 8192], P('tp', 'ctx'), may hold values from -16 to 16
- short_key: bfloat16 [4096, 8192], P('tp', 'ctx'), may hold values from -6 to 6
- short_value: bfloat16 [4096, 8192], P('tp', 'ctx'), may hold values from -6 to 6
- short_taps: bfloat16 [4096, 128], P('tp'), may hold values from -0.5 to 0.5
- norm_gain: float32 [4096], P('tp'), may hold values from 0.1 to 1.9
- long_key: bfloat16 [4096, 8192], P('tp', 'ctx'), may hold values from -6 to 6
- long_query: bfloat16 [4096, 8192], P('tp', 'ctx'), may hold values from -6 to 6
- residues: float32 [16, 4096], P(None, 'tp'), may hold values from -1.5 to 1.5
- decay_rates: float32 [16, 4096], P(None, 'tp'), may hold values from 6.1035156e-05 to 0.05
Outputs:
- mixer_output: float32 [4096, 8192], P('tp', 'ctx')
All inputs are finite; a program needn't handle non-finite values.
Results may differ from a plain program's by a relative error of at most 0.0029.
Values may be sent and summed in bfloat16 or wider, within the bound.
A program may use at most 128 MiB of HBM per device.

v0:
```python
import jax
import jax.numpy as jnp
from jax import lax
from jax.sharding import PartitionSpec as P

D = 4096


highest = lax.Precision.HIGHEST


def carried_in(value, axis, join, neutral):
    count, mine = (lax.axis_size(axis), lax.axis_index(axis))
    pieces = jax.tree.map(lambda part: lax.all_gather(part, axis), value)
    so_far = jax.tree.map(
        lambda part, zero: jnp.full_like(part, 0) + jnp.asarray(zero, part.dtype), value, neutral
    )

    def step(position, so_far):
        longer = join(so_far, jax.tree.map(lambda part: part[position], pieces))
        return jax.tree.map(lambda new, old: jnp.where(position < mine, new, old), longer, so_far)

    return lax.fori_loop(0, count - 1, step, so_far)


def passed_along(value, axis, by):
    devices = lax.axis_size(axis)
    pairs = [(i, i + by) for i in range(devices) if 0 <= i + by < devices]
    return lax.ppermute(value, axis, pairs)


def make_band(filter_taps):
    tap_count = filter_taps.shape[1]
    row_index = jnp.arange(tap_count)[:, None]
    col_index = jnp.arange(2 * tap_count)[None, :]
    lag_index = row_index + tap_count - col_index
    inside = (lag_index >= 0) & (lag_index < tap_count)
    picked = jnp.take(filter_taps, jnp.clip(lag_index, 0, tap_count - 1), axis=1)
    return jnp.where(inside[None, :, :], picked, jnp.zeros_like(picked))


def lower_band(kernel):
    block_len = kernel.shape[1]
    lag_index = jnp.arange(block_len)[:, None] - jnp.arange(block_len)[None, :]
    picked = jnp.take(kernel, jnp.clip(lag_index, 0, block_len - 1), axis=1)
    return jnp.where((lag_index >= 0)[None, :, :], picked, jnp.zeros_like(picked))


def short_block(extended, filter_taps):
    tap_count = filter_taps.shape[1]
    channels, span_len = extended.shape
    length = span_len - tap_count
    block_count = length // tap_count
    earlier = extended[:, :length].reshape(channels, block_count, tap_count)
    current = extended[:, tap_count:].reshape(channels, block_count, tap_count)
    windows = jnp.concatenate([earlier, current], axis=2)
    band_rows = make_band(filter_taps)
    mixed = jnp.einsum("cbm,cim->cbi", windows, band_rows, preferred_element_type=jnp.float32)
    return mixed.reshape(channels, length)


def carry_combine(earlier, following):
    return (earlier[0] * following[0], earlier[1] * following[0] + following[1])


def recurrent_mix(signal, residue, decays, block_len):
    channels, local_len = signal.shape
    block_count = local_len // block_len
    offsets = jnp.arange(block_len).astype(jnp.float32)
    weights = residue * jnp.sqrt(-jnp.expm1(-2.0 * decays))
    powers = jnp.exp(-decays[:, :, None] * offsets[None, None, :])
    kernel = jnp.einsum("mc,mct->ct", weights, powers, precision=highest)
    band_lower = lower_band(kernel)
    pieces = signal.reshape(channels, block_count, block_len)
    inner_part = jnp.einsum("cbj,cij->cbi", pieces, band_lower, precision=highest)
    tail_powers = jnp.flip(powers, axis=2)
    block_ends = jnp.einsum("mcj,cbj->mcb", tail_powers, pieces, precision=highest)
    step_index = jnp.arange(block_count)
    gap_index = step_index[:, None] - 1 - step_index[None, :]
    gap_decay = jnp.exp(
        -decays[:, :, None, None]
        * (block_len * jnp.maximum(gap_index, 0)).astype(jnp.float32)[None, None]
    )
    carry_matrix = jnp.where((gap_index >= 0)[None, None], gap_decay, jnp.zeros_like(gap_decay))
    incoming = jnp.einsum("mcbk,mck->mcb", carry_matrix, block_ends, precision=highest)
    device_state = jnp.exp(-decays * block_len) * incoming[:, :, -1] + block_ends[:, :, -1]
    device_decay = jnp.exp(-decays * local_len)
    entering = carried_in(
        (device_decay, device_state),
        "ctx",
        carry_combine,
        (jnp.ones_like(device_decay), jnp.zeros_like(device_state)),
    )[1]
    start_powers = jnp.exp(
        -decays[:, :, None] * (block_len * step_index).astype(jnp.float32)[None, None, :]
    )
    before = incoming + start_powers * entering[:, :, None]
    carried_part = jnp.einsum(
        "mcb,mci->cbi",
        before * weights[:, :, None],
        powers * jnp.exp(-decays)[:, :, None],
        precision=highest,
    )
    return (inner_part + carried_part).reshape(channels, local_len)


def shards(
    short_query,
    short_key,
    short_value,
    short_taps,
    norm_gain,
    long_key,
    long_query,
    residues,
    decay_rates,
):
    tap_count = short_taps.shape[1]
    channels, local_len = short_value.shape
    first_product = (short_key.astype(jnp.float32) * short_value.astype(jnp.float32)).astype(
        jnp.bfloat16
    )
    previous = passed_along(first_product[:, local_len - tap_count :], "ctx", 1)
    extended = jnp.concatenate([previous, first_product], axis=1)
    short_mix = short_block(extended, short_taps)
    gated = short_query.astype(jnp.float32) * short_mix
    squares = lax.psum(jnp.sum(gated * gated, axis=0), "tp")
    normed = gated * norm_gain[:, None] * lax.rsqrt(squares / D + 1e-06)[None, :]
    long_input = long_key.astype(jnp.float32) * normed
    long_mix = recurrent_mix(long_input, residues, decay_rates, tap_count)
    return long_query.astype(jnp.float32) * long_mix


def solution(mesh):
    in_specs = (
        P("tp", "ctx"),
        P("tp", "ctx"),
        P("tp", "ctx"),
        P("tp", None),
        P("tp"),
        P("tp", "ctx"),
        P("tp", "ctx"),
        P(None, "tp"),
        P(None, "tp"),
    )
    out_specs = P("tp", "ctx")
    return jax.shard_map(shards, mesh=mesh, in_specs=in_specs, out_specs=out_specs, check_vma=False)
```

profile of v0, /device:TPU:0, one launch (start us, length us, event | category | flops | bytes accessed | tf_op | source)
XLA Modules:
  0.0 462.1 jit_solution(15190103897317602908)
XLA Ops:
  0.0 3.0 multiply_convert_fusion
  3.1 4.8 %collective-permute-start = (bf16[512,128]{1,0:T(8,128)(2,1)S(1)}, bf16[512,128]{1,0:T(8,128)(2,1)S(1)}, u32[]{:S(2)}, u32[]{:S(2)}) collective-permute-start(bf16[512,128]{1,0:T(8,128)(2,1)S(1)} %slice.20), channel_id=1, source_target_pairs={{0,8},{8,16},{16,24},{1,9},{9,17},{17,25},{2,10},{10,18},{18,26},{... | collective-permute-start | bytes 393224 | tf_op jit(solution)/shard_map/ppermute | solution.py:29
  8.2 0.7 multiply_convert_fusion.1
  8.9 0.6 fusion.44
  9.6 0.7 fusion.37
  10.5 3.5 multiply_exponential_fusion
  14.7 131.7 %gather_fusion = bf16[32768,512]{1,0:T(8,128)(2,1)} fusion(bf16[512,128]{0,1:T(8,128)(2,1)S(1)} %copy.50, s32[32768]{0:T(1024)S(1)} %broadcast_clamp_fusion), kind=kCustom, calls=%fused_computation | custom fusion | bytes 67239936 | tf_op jit(solution)/shard_map/jit(_take)/gather | solution.py:38
  146.4 45.3 %copy.51 = bf16[128,256,512]{1,0,2:T(8,128)(2,1)} copy(bf16[128,256,512]{2,1,0:T(8,128)(2,1)} %bitcast.72) | data formatting | bytes 67108864 | tf_op jit(solution)/shard_map/jit(_take)/gather | solution.py:38
  191.7 1.9 copy.75
  193.6 7.2 %rev.4 = f32[16,512,128]{2,0,1:T(8,128)} reverse(f32[16,512,128]{2,0,1:T(8,128)} %multiply_exponential_fusion), dimensions={2} | reverse | bytes 8388608 | tf_op jit(solution)/shard_map/jit(_flip)/rev | solution.py:76
  200.9 0.6 fusion.38
  201.8 2.0 copy.74
  203.7 15.4 %fusion.3 = f32[512,16,128]{2,1,0:T(8,128)S(1)} fusion(bf16[128,256,512]{1,0,2:T(8,128)(2,1)} %copy.51, pred[128,256]{1,0:T(8,128)(4,1)S(1)} %get-tuple-element.138, pred[128,256]{1,0:T(8,128)(4,1)S(1)} %get-tuple-element.137, bf16[512,16,128]{2,1,0:T(8,128)(2,1)} %bitcast.81, bf16[512,16,128]{2,1,0:T(8,128)(2,1)} %bitcast.82), kind=kOutput, calls=%fused_computation.7 | convolution fusion | flops 578813952 | bytes 42008576 | tf_op jit(solution)/shard_map/cbm,cim->cbi/dot_general | solution.py:58
  219.1 2.0 copy-done.2
  221.2 3.9 multiply_reduce_fusion.2
  225.1 16.8 %psum.7 = f32[2048]{0:T(1024)S(1)} all-reduce(f32[2048]{0:T(1024)S(1)} %multiply_reduce_fusion.2), channel_id=1, replica_groups=mesh['ctx'=4,'tp'=8] {'tp'}, use_global_device_ids=true, to_apply=%region_1.2 | all-reduce | flops 2048 | bytes 16384 | tf_op jit(solution)/shard_map/psum | solution.py:127
  242.0 6.0 %multiply_bitcast_fusion = f32[64,8,16,128]{3,1,2,0:T(8,128)S(1)} fusion(bf16[512,2048]{1,0:T(8,128)(2,1)} %param.16, f32[64,8,16,128]{3,2,1,0:T(8,128)} %bitcast.79, bf16[512,2048]{1,0:T(8,128)(2,1)} %param.11, f32[2048]{0:T(1024)S(1)} %add_rsqrt_fusion, f32[512]{0:T(512)S(1)} %copy-done.18), kind=kLoop, calls=%fused_computation.31 | loop fusion | flops 6291456 | bytes 12593152
  248.0 0.9 copy.78
  249.0 2.0 copy-done
  251.0 8.1 %fusion.50 = f32[512,16,16]{2,1,0:T(8,128)} fusion(f32[512,16,128]{2,1,0:T(8,128)S(1)} %bitcast.74, f32[16,512,128]{2,0,1:T(8,128)S(1)} %copy-done.1), kind=kOutput, calls=%fused_computation.81 | convolution fusion | flops 201326592 | bytes 8912896 | tf_op jit(solution)/shard_map/mcj,cbj->mcb/dot_general | solution.py:77
  259.1 2.8 copy.54
  262.0 3.0 copy.72
  265.0 2.8 multiply_reduce_fusion
  268.3 6.0 %multiply_reduce_fusion.1 = f32[512,128]{1,0:T(8,128)S(1)} fusion(f32[512,16]{1,0:T(8,128)S(1)} %copy.71, f32[128]{0:T(128)S(1)} %copy-done.20, f32[16,512]{0,1:T(8,128)S(1)} %copy-done.5), kind=kLoop, calls=%fused_computation.27 | loop fusion | flops 3080192 | bytes 328192
  274.4 64.4 %gather_fusion.1 = f32[16384,512]{1,0:T(8,128)} fusion(f32[512,128]{0,1:T(8,128)S(1)} %copy.62, s32[16384]{0:T(1024)S(1)} %copy-done.10), kind=kCustom, calls=%fused_computation.1 | custom fusion | bytes 67174400 | tf_op jit(solution)/shard_map/jit(_take)/gather | solution.py:45
  338.8 35.6 %copy.53 = f32[128,128,512]{1,0,2:T(8,128)} copy(f32[128,128,512]{2,1,0:T(8,128)} %bitcast.73) | data formatting | bytes 67108864 | tf_op jit(solution)/shard_map/jit(_take)/gather | solution.py:45
  374.4 8.6 %all-gather = f32[64,512]{1,0:T(8,128)S(1)} all-gather(f32[16,512]{1,0:T(8,128)S(1)} %get-tuple-element.134), channel_id=2, replica_groups=mesh['ctx'=4,'tp'=8] {'ctx'}, dimensions={0}, use_global_device_ids=true | all-gather | bytes 163840 | tf_op jit(solution)/shard_map/all_gather | solution.py:14
  383.0 7.5 %all-gather.1 = f32[64,512]{1,0:T(8,128)S(1)} all-gather(f32[16,512]{1,0:T(8,128)S(1)} %get-tuple-element.135), channel_id=3, replica_groups=mesh['ctx'=4,'tp'=8] {'ctx'}, dimensions={0}, use_global_device_ids=true | all-gather | bytes 163840 | tf_op jit(solution)/shard_map/all_gather | solution.py:14
  391.2 3.7 copy.56
  395.0 56.4 %fusion.1 = f32[512,16,128]{2,1,0:T(8,128)S(1)} fusion(f32[512,16,128]{2,1,0:T(8,128)} %bitcast.75, f32[128,128,512]{1,0,2:T(8,128)} %copy.53, pred[128,128]{1,0:T(8,128)(4,1)S(1)} %copy-done.11, pred[128,128]{1,0:T(8,128)(4,1)S(1)} %copy-done.12), kind=kOutput, calls=%fused_computation.5 | convolution fusion | flops 1627389952 | bytes 41975808 | tf_op jit(solution)/shard_map/cbj,cij->cbi/dot_general | solution.py:75
  451.4 6.0 %fusion.22 = f32[512,16,128]{2,1,0:T(8,128)S(1)} fusion(f32[512,16,128]{2,1,0:T(8,128)S(1)} %fusion.1, f32[16,512,16]{0,2,1:T(8,128)S(1)} %copy-done.3, f32[16,512]{0,1:T(8,128)S(1)} %copy.55, f32[128]{0:T(128)S(1)} %copy-done.20, f32[16,512]{0,1:T(8,128)S(1)} %copy-done.5), kind=kOutput, calls=%fused_computation.34 | convolution fusion | flops 204472320 | bytes 8978944 | tf_op jit(solution)/shard_map/mcb,mci->cbi/dot_general | solution.py:98
  457.5 4.2 bitcast_multiply_fusion.1
  (70 shorter events, 3.0 us)
Async XLA Ops:
  0.0 10.3 %copy-start.14 = (f32[16,512]{1,0:T(8,128)S(1)}, f32[16,512]{1,0:T(8,128)}, u32[]{:S(2)}) copy-start(f32[16,512]{1,0:T(8,128)} %param.19) | copy-start | bytes 98308
  3.0 11.5 %copy-start.13 = (bf16[512,128]{1,0:T(8,128)(2,1)S(1)}, bf16[512,128]{1,0:T(8,128)(2,1)}, u32[]{:S(2)}) copy-start(bf16[512,128]{1,0:T(8,128)(2,1)} %param.14) | copy-start | bytes 393220
  3.1 198.4 %collective-permute-start = (bf16[512,128]{1,0:T(8,128)(2,1)S(1)}, bf16[512,128]{1,0:T(8,128)(2,1)S(1)}, u32[]{:S(2)}, u32[]{:S(2)}) collective-permute-start(bf16[512,128]{1,0:T(8,128)(2,1)S(1)} %slice.20), channel_id=1, source_target_pairs={{0,8},{8,16},{16,24},{1,9},{9,17},{17,25},{2,10},{10,18},{18,26},{... | collective-permute-start | bytes 393224 | tf_op jit(solution)/shard_map/ppermute | solution.py:29
  8.2 6.3 %copy-start.19 = (f32[128]{0:T(128)}, f32[128]{0:T(128)S(1)}, u32[]{:S(2)}) copy-start(f32[128]{0:T(128)S(1)} %iota_convert_fusion) | copy-start | bytes 1540
  10.4 4.2 copy-start.8
  10.5 135.9 %copy-start.4 = (f32[16,512]{0,1:T(8,128)}, f32[16,512]{0,1:T(8,128)S(1)}, u32[]{:S(2)}) copy-start(f32[16,512]{0,1:T(8,128)S(1)} %copy.52) | copy-start | bytes 98308
  219.1 2.0 copy-start.2
  219.1 22.8 %copy-start.18 = (f32[512]{0:T(512)S(1)}, f32[512]{0:T(512)}, u32[]{:S(2)}) copy-start(f32[512]{0:T(512)} %param.15) | copy-start | bytes 6148
  248.0 3.0 copy-start.1
  248.9 2.0 copy-start
  259.1 5.9 %copy-start.9 = (f32[16,512]{1,0:T(8,128)S(1)}, f32[16,512]{1,0:T(8,128)}, u32[]{:S(2)}) copy-start(f32[16,512]{1,0:T(8,128)} %copy-done.8) | copy-start | bytes 98308
  259.1 5.9 %copy-start.17 = (f32[16,16]{1,0:T(8,128)S(1)}, f32[16,16]{1,0:T(8,128)}, u32[]{:S(2)}) copy-start(f32[16,16]{1,0:T(8,128)} %multiply_convert_fusion.1) | copy-start | bytes 3076
  259.1 5.9 %copy-start.21 = (pred[16,16]{1,0:T(8,128)(4,1)S(1)}, pred[16,16]{1,0:T(8,128)(4,1)}, u32[]{:S(2)}) copy-start(pred[16,16]{1,0:T(8,128)(4,1)} %fusion.44) | copy-start | bytes 772
  261.9 6.2 %copy-start.15 = (f32[16,512]{1,0:T(8,128)S(1)}, f32[16,512]{1,0:T(8,128)}, u32[]{:S(2)}) copy-start(f32[16,512]{1,0:T(8,128)} %param.19) | copy-start | bytes 98308
  261.9 6.2 %copy-start.16 = (f32[16,512]{1,0:T(8,128)S(1)}, f32[16,512]{1,0:T(8,128)}, u32[]{:S(2)}) copy-start(f32[16,512]{1,0:T(8,128)} %param.18) | copy-start | bytes 98308
  261.9 6.4 %copy-start.5 = (f32[16,512]{0,1:T(8,128)S(1)}, f32[16,512]{0,1:T(8,128)}, u32[]{:S(2)}) copy-start(f32[16,512]{0,1:T(8,128)} %copy-done.4) | copy-start | bytes 98308
  262.0 6.4 %copy-start.20 = (f32[128]{0:T(128)S(1)}, f32[128]{0:T(128)}, u32[]{:S(2)}) copy-start(f32[128]{0:T(128)} %copy-done.19) | copy-start | bytes 1540
  265.0 9.4 %copy-start.10 = (s32[16384]{0:T(1024)S(1)}, s32[16384]{0:T(1024)}, u32[]{:S(2)}) copy-start(s32[16384]{0:T(1024)} %fusion.37) | copy-start | bytes 196612
  338.8 51.6 %copy-start.7 = (f32[16,512]{1,0:T(8,128)S(1)}, f32[16,512]{1,0:T(8,128)}, u32[]{:S(2)}) copy-start(f32[16,512]{1,0:T(8,128)} %custom-call) | copy-start | bytes 98308
  338.8 52.0 %copy-start.22 = (f32[16]{0:T(128)S(1)}, f32[16]{0:T(128)}, u32[]{:S(2)}) copy-start(f32[16]{0:T(128)} %multiply_convert_fusion.2) | copy-start | bytes 196
  374.4 20.6 %copy-start.11 = (pred[128,128]{1,0:T(8,128)(4,1)S(1)}, pred[128,128]{1,0:T(8,128)(4,1)}, u32[]{:S(2)}) copy-start(pred[128,128]{1,0:T(8,128)(4,1)} %get-tuple-element.139) | copy-start | bytes 49156
  374.4 20.6 %copy-start.12 = (pred[128,128]{1,0:T(8,128)(4,1)S(1)}, pred[128,128]{1,0:T(8,128)(4,1)}, u32[]{:S(2)}) copy-start(pred[128,128]{1,0:T(8,128)(4,1)} %get-tuple-element.140) | copy-start | bytes 49156
  395.0 56.4 %copy-start.3 = (f32[16,512,16]{0,2,1:T(8,128)S(1)}, f32[16,512,16]{0,2,1:T(8,128)}, u32[]{:S(2)}) copy-start(f32[16,512,16]{0,2,1:T(8,128)} %copy.56) | copy-start | bytes 1572868
  451.4 6.0 %copy-start.6 = (bf16[512,2048]{1,0:T(8,128)(2,1)S(1)}, bf16[512,2048]{1,0:T(8,128)(2,1)}, u32[]{:S(2)}) copy-start(bf16[512,2048]{1,0:T(8,128)(2,1)} %param.17) | copy-start | bytes 6291460
where the time goes:
time: 471 us; the launch traced here: 462 us
  local copies, waits for them, and re-layouts  304 us (65%)
  matrix products  85.9 us (18%)
  other arithmetic  33.6 us (7%)
  blocking collectives  32.9 us (7%)
  starting transfers between devices  4.85 us (1%)
    gather x2, local copies, waits for them, and re-layouts, make_band(): jnp.take(filter_taps, jnp.clip(lag_index, 0, tap_count - 1), axis=1)  177 us
    gather x2, local copies, waits for them, and re-layouts, lower_band(): picked = jnp.take(kernel, jnp.clip(lag_index, 0, block_len - 1), axis=1)  100 us
    dot_general x1, matrix products, recurrent_mix(): jnp.einsum('cbj,cij->cbi', pieces, band_lower, precision=highest)  56.4 us
    psum x1, blocking collectives, shards(): squares = lax.psum(jnp.sum(gated * gated, axis=0), 'tp')  16.8 us
    all_gather x2, blocking collectives, carried_in(): pieces = jax.tree.map(lambda part: lax.all_gather(part, axis), value)  16 us
    dot_general x1, matrix products, short_block(): jnp.einsum('cbm,cim->cbi', windows, band_rows, preferred_element_type=jnp...  15.4 us
    unnamed x6, other arithmetic  15.1 us
    unnamed x53, local copies, waits for them, and re-layouts  12.3 us
  transfers between devices with their start and end apart: 1, of which 0 were waited for; matrix products, arithmetic and copies ran while one was open for 42% of the time, Pallas kernels for 0%

commit v1 on v0

v1 whole, which is shorter than its diff:
```python
import functools

import jax
import jax.numpy as jnp
from jax import lax
from jax.experimental import pallas as pl
from jax.experimental.pallas import tpu as pltpu
from jax.sharding import PartitionSpec as P

F32 = jnp.float32
BF16 = jnp.bfloat16
SUB = 8


def fused(
    n_ctx,
    n_tp,
    width,
    sq_hbm,
    sk_hbm,
    sv_hbm,
    lk_hbm,
    lq_hbm,
    taps_ref,
    gain_ref,
    decay_ref,
    weight_ref,
    out_hbm,
    sq,
    sk,
    sv,
    lk,
    lq,
    key_edge,
    value_edge,
    edge_send,
    edge_recv,
    gated,
    squares,
    sums,
    signal,
    tails,
    heads,
    bands,
    carry,
    states,
    in_sem,
    edge_in_sem,
    out_sem,
    edge_sem,
    sum_send_sem,
    sum_recv_sem,
    state_send_sem,
    state_recv_sem,
):
    channels, length = gated.shape
    block = taps_ref.shape[1]
    blocks = length // block
    groups = channels // SUB
    chunks = in_sem.shape[1]
    chunk_rows = channels // chunks
    pairs = chunk_rows // 16
    my_ctx = lax.axis_index("ctx")
    my_tp = lax.axis_index("tp")

    def edge_in(which, source, target):
        return pltpu.make_async_copy(
            source.at[:, pl.ds(length - block, block)], target, edge_in_sem.at[which]
        )

    def bring(which, source, target, chunk):
        rows = pl.ds(pl.multiple_of(chunk * chunk_rows, 16), chunk_rows)
        return pltpu.make_async_copy(source.at[rows], target.at[rows], in_sem.at[which, chunk])

    edge_in(0, sk_hbm, key_edge).start()
    edge_in(1, sv_hbm, value_edge).start()

    def start_short(chunk, _):
        bring(0, sk_hbm, sk, chunk).start()
        bring(1, sv_hbm, sv, chunk).start()
        bring(2, sq_hbm, sq, chunk).start()
        return 0

    def start_long(chunk, _):
        bring(3, lk_hbm, lk, chunk).start()
        bring(4, lq_hbm, lq, chunk).start()
        return 0

    lax.fori_loop(0, chunks, start_short, 0)
    lax.fori_loop(0, chunks, start_long, 0)

    barrier = pltpu.get_barrier_semaphore()

    def greet_ctx(step, _):
        other = lax.rem(my_ctx + step, n_ctx)
        pl.semaphore_signal(
            barrier, inc=1, device_id={"ctx": other}, device_id_type=pl.DeviceIdType.MESH
        )
        return 0

    def greet_tp(step, _):
        other = lax.rem(my_tp + step, n_tp)
        pl.semaphore_signal(
            barrier, inc=1, device_id={"tp": other}, device_id_type=pl.DeviceIdType.MESH
        )
        return 0

    lax.fori_loop(1, n_ctx, greet_ctx, 0)
    lax.fori_loop(1, n_tp, greet_tp, 0)
    pl.semaphore_wait(barrier, n_ctx + n_tp - 2)

    edge_in(0, sk_hbm, key_edge).wait()
    edge_in(1, sv_hbm, value_edge).wait()
    edge_send[...] = (key_edge[...].astype(F32) * value_edge[...].astype(F32)).astype(BF16)
    edge_copy = pltpu.make_async_remote_copy(
        src_ref=edge_send,
        dst_ref=edge_recv,
        send_sem=edge_sem.at[0],
        recv_sem=edge_sem.at[1],
        device_id={"ctx": lax.rem(my_ctx + 1, n_ctx)},
        device_id_type=pl.DeviceIdType.MESH,
    )
    edge_copy.start()

    row_id = lax.broadcasted_iota(jnp.int32, (block, block), 0)
    col_id = lax.broadcasted_iota(jnp.int32, (block, block), 1)
    lower_mask = jnp.where(col_id >= row_id, 1.0, 0.0).astype(BF16)
    upper_mask = jnp.where(col_id < row_id, 1.0, 0.0).astype(BF16)
    pick_row = lax.broadcasted_iota(jnp.int32, (16, block), 0) % SUB
    row_masks = [jnp.where(pick_row == c, 1.0, 0.0).astype(BF16) for c in range(SUB)]
    sub_id = lax.broadcasted_iota(jnp.int32, (SUB, block), 0)
    lane_id = lax.broadcasted_iota(jnp.int32, (SUB, block), 1)
    own_modes = (lane_id // (block // SUB)) == sub_id

    def spread(stacked):
        rows = stacked.shape[0]
        tiled = stacked.reshape(rows // 16, 16, block)
        return jnp.concatenate(
            [(tiled * row_masks[c][None]).reshape(rows, block) for c in range(SUB)], axis=1
        )

    def circulant(row):
        whole = jnp.broadcast_to(row, (block, block))
        return pltpu.roll(whole, 0, 1, stride=1, stride_axis=0).astype(BF16)

    def parts(value):
        high = value.astype(BF16)
        return high, (value - high.astype(F32)).astype(BF16)

    def at(b):
        return slice(b * block, (b + 1) * block)

    def over(b):
        return slice(b * SUB, (b + 1) * SUB)

    squares[...] = jnp.zeros_like(squares)
    edge_copy.wait()
    has_left = jnp.where(my_ctx > 0, 1.0, 0.0).astype(F32)

    def short_pair(pair, _):
        rows = pl.ds(pl.multiple_of(pair * 16, 16), 16)
        product = sk[rows, :].astype(F32) * sv[rows, :].astype(F32)
        query = sq[rows, :].astype(F32)
        edge = edge_recv[rows, :].astype(F32) * has_left
        taps = taps_ref[rows, :].astype(F32)
        for half in range(2):
            own = slice(half * SUB, (half + 1) * SUB)
            stacked = jnp.concatenate(
                [edge[own]]
                + [product[own, at(b)] for b in range(blocks)]
                + [jnp.zeros((SUB, block), F32)],
                axis=0,
            ).astype(BF16)
            bands_now = []
            for c in range(SUB):
                turned = circulant(taps[half * SUB + c : half * SUB + c + 1])
                bands_now.append(
                    jnp.concatenate([turned * lower_mask, turned * upper_mask], axis=1)
                )
            mixed = jnp.dot(
                spread(stacked),
                jnp.concatenate(bands_now, axis=0),
                preferred_element_type=F32,
            )
            place = pl.ds(pl.multiple_of(pair * 16 + half * SUB, SUB), SUB)
            for b in range(blocks):
                mix = mixed[over(b + 1), :block] + mixed[over(b), block:]
                gate = query[own, at(b)] * mix
                gated[place, at(b)] = gate
                squares[:, at(b)] += gate * gate
        return 0

    def short_chunk(chunk, _):
        bring(0, sk_hbm, sk, chunk).wait()
        bring(1, sv_hbm, sv, chunk).wait()
        bring(2, sq_hbm, sq, chunk).wait()
        lax.fori_loop(chunk * pairs, (chunk + 1) * pairs, short_pair, 0)
        return 0

    lax.fori_loop(0, chunks, short_chunk, 0)

    sums[my_tp] = jnp.sum(squares[...], axis=0, keepdims=True)

    def sum_copy(slot, other):
        return pltpu.make_async_remote_copy(
            src_ref=sums.at[slot],
            dst_ref=sums.at[slot],
            send_sem=sum_send_sem.at[other],
            recv_sem=sum_recv_sem.at[slot],
            device_id={"tp": other},
            device_id_type=pl.DeviceIdType.MESH,
        )

    def sum_start(step, _):
        sum_copy(my_tp, lax.rem(my_tp + step, n_tp)).start()
        return 0

    lax.fori_loop(1, n_tp, sum_start, 0)

    step_at = col_id.astype(F32)

    def make_params(g, _):
        decay = jnp.broadcast_to(decay_ref[pl.ds(g, 1), :], (block, block)).T
        weight = jnp.broadcast_to(weight_ref[pl.ds(g, 1), :], (block, block)).T
        tails[g] = jnp.concatenate(parts(jnp.exp(-decay * (block - 1 - step_at))), axis=1)
        kernel = weight * jnp.exp(-decay * step_at)
        high, low = parts(weight * jnp.exp(-decay * (step_at + 1.0)))
        heads[g] = jnp.concatenate([high, high, low], axis=0)
        modes = block // SUB
        for c in range(SUB):
            row = jnp.sum(kernel[c * modes : (c + 1) * modes], axis=0, keepdims=True)
            bands[g, c * block : (c + 1) * block, :] = circulant(row) * lower_mask
        return 0

    lax.fori_loop(0, groups, make_params, 0)

    def sum_wait(step, _):
        other = lax.rem(my_tp + step, n_tp)
        sum_copy(my_tp, other).wait_send()
        sum_copy(other, other).wait_recv()
        return 0

    lax.fori_loop(1, n_tp, sum_wait, 0)
    total = sums[0]
    for other in range(1, n_tp):
        total = total + sums[other]
    squares[...] = jnp.broadcast_to(lax.rsqrt(total / width + 1e-06), squares.shape)

    def state_pair(pair, _):
        rows = pl.ds(pl.multiple_of(pair * 16, 16), 16)
        key = lk[rows, :].astype(F32)
        for half in range(2):
            own = slice(half * SUB, (half + 1) * SUB)
            g = pair * 2 + half
            place = pl.ds(pl.multiple_of(pair * 16 + half * SUB, SUB), SUB)
            gain = gain_ref[place, :]
            stacked = jnp.concatenate(
                [
                    key[own, at(b)] * (gated[place, at(b)] * gain * squares[:, at(b)])
                    for b in range(blocks)
                ],
                axis=0,
            ).astype(BF16)
            signal[g] = stacked
            ends = lax.dot_general(
                jnp.concatenate([stacked, stacked], axis=1),
                tails[g],
                (((1,), (1,)), ((), ())),
                preferred_element_type=F32,
            )
            fade = jnp.exp(-decay_ref[pl.ds(g, 1), :] * block)
            state = jnp.zeros((SUB, block), F32)
            for b in range(blocks):
                carry[g, over(b), :] = state
                state = fade * state + jnp.where(own_modes, ends[over(b)], 0.0)
            states[my_ctx, pl.ds(g, 1), :] = jnp.sum(state, axis=0, keepdims=True)
        return 0

    def state_chunk(chunk, _):
        bring(3, lk_hbm, lk, chunk).wait()
        lax.fori_loop(chunk * pairs, (chunk + 1) * pairs, state_pair, 0)
        return 0

    lax.fori_loop(0, chunks, state_chunk, 0)

    def state_copy(slot, other):
        return pltpu.make_async_remote_copy(
            src_ref=states.at[slot],
            dst_ref=states.at[slot],
            send_sem=state_send_sem.at[other],
            recv_sem=state_recv_sem.at[slot],
            device_id={"ctx": other},
            device_id_type=pl.DeviceIdType.MESH,
        )

    def state_start(step, _):
        state_copy(my_ctx, lax.rem(my_ctx + step, n_ctx)).start()
        return 0

    lax.fori_loop(1, n_ctx, state_start, 0)

    def inner_group(g, _):
        place = pl.ds(pl.multiple_of(g * SUB, SUB), SUB)
        inner = jnp.dot(spread(signal[g]), bands[g], preferred_element_type=F32)
        for b in range(blocks):
            gated[place, at(b)] = inner[over(b)]
        return 0

    lax.fori_loop(0, groups, inner_group, 0)

    def state_wait(step, _):
        other = lax.rem(my_ctx + step, n_ctx)
        state_copy(my_ctx, other).wait_send()
        state_copy(other, other).wait_recv()
        return 0

    lax.fori_loop(1, n_ctx, state_wait, 0)

    entering = jnp.zeros(decay_ref.shape, F32)
    device_fade = jnp.exp(-decay_ref[...] * length)
    for other in range(n_ctx - 1):
        further = device_fade * entering + states[other]
        entering = jnp.where(other < my_ctx, further, entering)
    states[0] = entering

    def out_copy(chunk):
        rows = pl.ds(pl.multiple_of(chunk * chunk_rows, 16), chunk_rows)
        return pltpu.make_async_copy(gated.at[rows], out_hbm.at[rows], out_sem.at[chunk])

    def last_pair(pair, _):
        rows = pl.ds(pl.multiple_of(pair * 16, 16), 16)
        query = lq[rows, :].astype(F32)
        for half in range(2):
            own = slice(half * SUB, (half + 1) * SUB)
            g = pair * 2 + half
            place = pl.ds(pl.multiple_of(pair * 16 + half * SUB, SUB), SUB)
            fade = jnp.exp(-decay_ref[pl.ds(g, 1), :] * block)
            here = jnp.where(own_modes, states[0, pl.ds(g, 1), :], 0.0)
            before = []
            for b in range(blocks):
                before.append(carry[g, over(b), :] + here)
                here = here * fade
            high, low = parts(jnp.concatenate(before, axis=0))
            carried = jnp.dot(
                jnp.concatenate([high, low, high], axis=1),
                heads[g],
                preferred_element_type=F32,
            )
            for b in range(blocks):
                gated[place, at(b)] = query[own, at(b)] * (gated[place, at(b)] + carried[over(b)])
        return 0

    def last_chunk(chunk, _):
        bring(4, lq_hbm, lq, chunk).wait()
        lax.fori_loop(chunk * pairs, (chunk + 1) * pairs, last_pair, 0)
        out_copy(chunk).start()
        return 0

    lax.fori_loop(0, chunks, last_chunk, 0)

    def out_wait(chunk, _):
        out_copy(chunk).wait()
        return 0

    lax.fori_loop(0, chunks, out_wait, 0)


def shards(
    short_query,
    short_key,
    short_value,
    short_taps,
    norm_gain,
    long_key,
    long_query,
    residues,
    decay_rates,
):
    channels, length = short_value.shape
    block = short_taps.shape[1]
    modes = decay_rates.shape[0]
    groups = channels // SUB
    assert modes * SUB == block
    n_ctx, n_tp = lax.axis_size("ctx"), lax.axis_size("tp")
    chunks = min(8, channels // 16)
    weights = residues * jnp.sqrt(-jnp.expm1(-2.0 * decay_rates))
    decays = decay_rates.T.reshape(groups, block)
    weights = weights.T.reshape(groups, block)
    gains = jnp.broadcast_to(norm_gain[:, None], (channels, block))
    hbm = pl.BlockSpec(memory_space=pl.ANY)
    vmem = pl.BlockSpec(memory_space=pltpu.VMEM)
    dma = pltpu.SemaphoreType.DMA
    return pl.pallas_call(
        functools.partial(fused, n_ctx, n_tp, channels * n_tp),
        out_shape=jax.ShapeDtypeStruct((channels, length), F32),
        in_specs=[hbm] * 5 + [vmem] * 4,
        out_specs=hbm,
        scratch_shapes=[pltpu.VMEM((channels, length), BF16)] * 5
        + [pltpu.VMEM((channels, block), BF16)] * 4
        + [
            pltpu.VMEM((channels, length), F32),
            pltpu.VMEM((SUB, length), F32),
            pltpu.VMEM((n_tp, 1, length), F32),
            pltpu.VMEM((groups, block, block), BF16),
            pltpu.VMEM((groups, block, 2 * block), BF16),
            pltpu.VMEM((groups, 3 * block, block), BF16),
            pltpu.VMEM((groups, SUB * block, block), BF16),
            pltpu.VMEM((groups, block, block), F32),
            pltpu.VMEM((n_ctx, groups, block), F32),
            dma((5, chunks)),
            dma((2,)),
            dma((chunks,)),
            dma((2,)),
            dma((n_tp,)),
            dma((n_tp,)),
            dma((n_ctx,)),
            dma((n_ctx,)),
        ],
        compiler_params=pltpu.CompilerParams(
            collective_id=0, has_side_effects=True, vmem_limit_bytes=56 * 1024 * 1024
        ),
    )(
        short_query,
        short_key,
        short_value,
        long_key,
        long_query,
        short_taps,
        gains,
        decays,
        weights,
    )


def solution(mesh):
    in_specs = (
        P("tp", "ctx"),
        P("tp", "ctx"),
        P("tp", "ctx"),
        P("tp", None),
        P("tp"),
        P("tp", "ctx"),
        P("tp", "ctx"),
        P(None, "tp"),
        P(None, "tp"),
    )
    out_specs = P("tp", "ctx")
    return jax.shard_map(shards, mesh=mesh, in_specs=in_specs, out_specs=out_specs, check_vma=False)
```

time: 471 us -> 79.6 us (0.17); the launches traced: 462 us -> 79.3 us
  local copies, waits for them, and re-layouts: 304 us -> 8.7 us
  matrix products: 85.9 us -> 0 us
  Pallas kernels: 0 us -> 69.7 us
  blocking collectives: 32.9 us -> 0 us
  other arithmetic: 33.6 us -> 0.8 us
  starting transfers between devices: 4.85 us -> 0 us
    gather x4 -> x0, local copies, waits for them, and re-layouts: 277 us -> none  [the longest x2 177 us: make_band(): jnp.take(filter_taps, jnp.clip(lag_index, 0, tap_count - 1), axis=1)]
    dot_general x4 -> x0, matrix products: 85.9 us -> none  [the longest x1 56.4 us: recurrent_mix(): jnp.einsum('cbj,cij->cbi', pieces, band_lower, precision=highest)]
    pallas_call x0 -> x1, Pallas kernels: none -> 69.7 us  [shards(): pl.pallas_call(functools.partial(fused, n_ctx, n_tp, channels * n_tp), ou...]
    psum x1 -> x0, blocking collectives: 16.8 us -> none  [shards(): squares = lax.psum(jnp.sum(gated * gated, axis=0), 'tp')]
    all_gather x2 -> x0, blocking collectives: 16 us -> none  [carried_in(): pieces = jax.tree.map(lambda part: lax.all_gather(part, axis), value)]
    unnamed x6 -> x0, other arithmetic: 15.1 us -> none
    unnamed x53 -> x1, local copies, waits for them, and re-layouts: 12.3 us -> 4.7 us
    rev x1 -> x0, local copies, waits for them, and re-layouts: 7.22 us -> none  [recurrent_mix(): tail_powers = jnp.flip(powers, axis=2)]
  transfers between devices with their start and end apart: 1 -> 0, of which waited for: 0 -> 0; matrix products, arithmetic and copies ran while one was open for 42% -> 0% of each run, Pallas kernels for 0% -> 0%
where the time goes in v1:
time: 79.6 us; the launch traced here: 79.3 us
  Pallas kernels  69.7 us (88%)
  local copies, waits for them, and re-layouts  8.7 us (11%)
  other arithmetic  0.8 us (1%)
    pallas_call x1, Pallas kernels, shards(): pl.pallas_call(functools.partial(fused, n_ctx, n_tp, channels * n_tp), ou...  69.7 us
    unnamed x1, local copies, waits for them, and re-layouts  4.7 us

profile of v1, /device:TPU:0, one launch (start us, length us, event | category | flops | bytes accessed | tf_op | source)
XLA Modules:
  0.0 79.3 jit_solution(17034272510452592103)
XLA Ops:
  0.0 0.8 %multiply_bitcast_fusion = f32[512,16]{0,1:T(8,128)S(1)} fusion(f32[16,512]{1,0:T(8,128)} %param.16, f32[16,512]{1,0:T(8,128)} %param.17), kind=kLoop, calls=%fused_computation | loop fusion | flops 24576 | bytes 98304 | tf_op jit(solution)/shard_map/transpose | solution.py:388
  0.8 0.1 copy.13
  0.9 0.7 reshape.8.weight_ref
  1.7 1.5 %broadcast_in_dim.2.gain_ref = f32[512,128]{1,0:T(8,128)} broadcast(f32[512]{0:T(512)} %param.13), dimensions={0} | broadcast | bytes 264192 | tf_op jit(solution)/shard_map/broadcast_in_dim | solution.py:389
  3.2 0.9 %copy.12 = f32[512,16]{1,0:T(8,128)S(1)} copy(f32[512,16]{0,1:T(8,128)} %bitcast.3) | data formatting | bytes 65536 | tf_op jit(solution)/shard_map/transpose | solution.py:387
  4.1 0.7 reshape.7.decay_ref
  4.8 69.7 %shard_map.91 = f32[512,2048]{1,0:T(8,128)} custom-call(bf16[512,2048]{1,0:T(8,128)(2,1)} %sq_hbm.1, bf16[512,2048]{1,0:T(8,128)(2,1)} %sk_hbm.1, bf16[512,2048]{1,0:T(8,128)(2,1)} %sv_hbm.1, bf16[512,2048]{1,0:T(8,128)(2,1)} %lk_hbm.1, bf16[512,2048]{1,0:T(8,128)(2,1)} %lq_hbm.1, bf16[512,128]{1,0:T(8,128)(2,1)} %taps_ref.1, ...), custom_call_target="tpu_custom_call" | custom-call | tf_op jit(solution)/shard_map/pallas_call | solution.py:393
  74.6 4.7 %copy.15 = f32[512,2048]{1,0:T(8,128)} copy(f32[512,2048]{1,0:T(8,128)} %shard_map.91) | data formatting | bytes 8388608

commit v2 on v1

--- a/solution.py
+++ b/solution.py
@@ -140,18 +140,46 @@
         )
 
     def circulant(row):
-        whole = jnp.broadcast_to(row, (block, block))
-        return pltpu.roll(whole, 0, 1, stride=1, stride_axis=0).astype(BF16)
+        base = jnp.broadcast_to(row, (16, block))
+        base = pltpu.roll(base, 0, 1, stride=1, stride_axis=0).astype(BF16)
+        turned = [base] + [pltpu.roll(base, 16 * a, 1) for a in range(1, block // 16)]
+        return jnp.concatenate(turned, axis=0)
 
     def parts(value):
         high = value.astype(BF16)
         return high, (value - high.astype(F32)).astype(BF16)
 
+    def run_pairs(chunk, body):
+        lax.fori_loop(
+            0, pairs, lambda i, _: body(chunk * pairs + i, 0), 0, unroll=min(2, pairs)
+        )
+
     def at(b):
         return slice(b * block, (b + 1) * block)
 
     def over(b):
         return slice(b * SUB, (b + 1) * SUB)
+
+    step_at = col_id.astype(F32)
+    modes = block // SUB
+
+    def make_params(step, _):
+        for g in [step * 4 + i for i in range(4)]:
+            decay = jnp.broadcast_to(decay_ref[pl.ds(g, 1), :], (block, block)).T
+            weight = jnp.broadcast_to(weight_ref[pl.ds(g, 1), :], (block, block)).T
+            tail = jnp.concatenate(parts(jnp.exp(-decay * (block - 1 - step_at))), axis=1)
+            kernel = weight * jnp.exp(-decay * step_at)
+            high, low = parts(weight * jnp.exp(-decay * (step_at + 1.0)))
+            band = []
+            for c in range(SUB):
+                row = jnp.sum(kernel[c * modes : (c + 1) * modes], axis=0, keepdims=True)
+                band.append(circulant(row) * lower_mask)
+            tails[g] = tail
+            heads[g] = jnp.concatenate([high, high, low], axis=0)
+            bands[g] = jnp.concatenate(band, axis=0)
+        return 0
+
+    lax.fori_loop(0, groups // 8, make_params, 0)
 
     squares[...] = jnp.zeros_like(squares)
     edge_copy.wait()
@@ -163,6 +191,7 @@
         query = sq[rows, :].astype(F32)
         edge = edge_recv[rows, :].astype(F32) * has_left
         taps = taps_ref[rows, :].astype(F32)
+        gates = []
         for half in range(2):
             own = slice(half * SUB, (half + 1) * SUB)
             stacked = jnp.concatenate(
@@ -182,19 +211,23 @@
                 jnp.concatenate(bands_now, axis=0),
                 preferred_element_type=F32,
             )
-            place = pl.ds(pl.multiple_of(pair * 16 + half * SUB, SUB), SUB)
-            for b in range(blocks):
-                mix = mixed[over(b + 1), :block] + mixed[over(b), block:]
-                gate = query[own, at(b)] * mix
-                gated[place, at(b)] = gate
-                squares[:, at(b)] += gate * gate
+            gates.append(
+                [
+                    query[own, at(b)] * (mixed[over(b + 1), :block] + mixed[over(b), block:])
+                    for b in range(blocks)
+                ]
+            )
+        for b in range(blocks):
+            first, second = gates[0][b], gates[1][b]
+            gated[rows, at(b)] = jnp.concatenate([first, second], axis=0)
+            squares[:, at(b)] += first * first + second * second
         return 0
 
     def short_chunk(chunk, _):
         bring(0, sk_hbm, sk, chunk).wait()
         bring(1, sv_hbm, sv, chunk).wait()
         bring(2, sq_hbm, sq, chunk).wait()
-        lax.fori_loop(chunk * pairs, (chunk + 1) * pairs, short_pair, 0)
+        run_pairs(chunk, short_pair)
         return 0
 
     lax.fori_loop(0, chunks, short_chunk, 0)
@@ -217,22 +250,7 @@
 
     lax.fori_loop(1, n_tp, sum_start, 0)
 
-    step_at = col_id.astype(F32)
-
-    def make_params(g, _):
-        decay = jnp.broadcast_to(decay_ref[pl.ds(g, 1), :], (block, block)).T
-        weight = jnp.broadcast_to(weight_ref[pl.ds(g, 1), :], (block, block)).T
-        tails[g] = jnp.concatenate(parts(jnp.exp(-decay * (block - 1 - step_at))), axis=1)
-        kernel = weight * jnp.exp(-decay * step_at)
-        high, low = parts(weight * jnp.exp(-decay * (step_at + 1.0)))
-        heads[g] = jnp.concatenate([high, high, low], axis=0)
-        modes = block // SUB
-        for c in range(SUB):
-            row = jnp.sum(kernel[c * modes : (c + 1) * modes], axis=0, keepdims=True)
-            bands[g, c * block : (c + 1) * block, :] = circulant(row) * lower_mask
-        return 0
-
-    lax.fori_loop(0, groups, make_params, 0)
+    lax.fori_loop(groups // 8, groups // 4, make_params, 0)
 
     def sum_wait(step, _):
         other = lax.rem(my_tp + step, n_tp)
@@ -278,7 +296,7 @@
 
     def state_chunk(chunk, _):
         bring(3, lk_hbm, lk, chunk).wait()
-        lax.fori_loop(chunk * pairs, (chunk + 1) * pairs, state_pair, 0)
+        run_pairs(chunk, state_pair)
         return 0
 
     lax.fori_loop(0, chunks, state_chunk, 0)
@@ -299,14 +317,17 @@
 
     lax.fori_loop(1, n_ctx, state_start, 0)
 
-    def inner_group(g, _):
-        place = pl.ds(pl.multiple_of(g * SUB, SUB), SUB)
-        inner = jnp.dot(spread(signal[g]), bands[g], preferred_element_type=F32)
+    def inner_groups(step, _):
+        inners = [
+            jnp.dot(spread(signal[step * 4 + i]), bands[step * 4 + i], preferred_element_type=F32)
+            for i in range(4)
+        ]
+        rows = pl.ds(pl.multiple_of(step * 4 * SUB, 4 * SUB), 4 * SUB)
         for b in range(blocks):
-            gated[place, at(b)] = inner[over(b)]
-        return 0
-
-    lax.fori_loop(0, groups, inner_group, 0)
+            gated[rows, at(b)] = jnp.concatenate([inner[over(b)] for inner in inners], axis=0)
+        return 0
+
+    lax.fori_loop(0, groups // 4, inner_groups, 0)
 
     def state_wait(step, _):
         other = lax.rem(my_ctx + step, n_ctx)
@@ -352,7 +373,7 @@
 
     def last_chunk(chunk, _):
         bring(4, lq_hbm, lq, chunk).wait()
-        lax.fori_loop(chunk * pairs, (chunk + 1) * pairs, last_pair, 0)
+        run_pairs(chunk, last_pair)
         out_copy(chunk).start()
         return 0
 

time: 79.6 us -> 65.7 us (0.83)
  Pallas kernels: 69.7 us -> 55.9 us
    pallas_call x1, Pallas kernels: 69.7 us -> 55.9 us  [shards(): pl.pallas_call(functools.partial(fused, n_ctx, n_tp, channels * n_tp), ou...]
where the time goes in v2:
time: 65.7 us; the launch traced here: 65.4 us
  Pallas kernels  55.9 us (85%)
  local copies, waits for them, and re-layouts  8.7 us (13%)
  other arithmetic  0.8 us (1%)
    pallas_call x1, Pallas kernels, shards(): pl.pallas_call(functools.partial(fused, n_ctx, n_tp, channels * n_tp), ou...  55.9 us
    unnamed x1, local copies, waits for them, and re-layouts  4.7 us
    broadcast_in_dim x1, local copies, waits for them, and re-layouts, shards(): gains = jnp.broadcast_to(norm_gain[:, None], (channels, block))  1.52 us

profile of v2, /device:TPU:0, one launch (start us, length us, event | category | flops | bytes accessed | tf_op | source)
XLA Modules:
  0.0 65.4 jit_solution(7424451465036297957)
XLA Ops:
  0.0 0.8 %multiply_bitcast_fusion = f32[512,16]{0,1:T(8,128)S(1)} fusion(f32[16,512]{1,0:T(8,128)} %param.16, f32[16,512]{1,0:T(8,128)} %param.17), kind=kLoop, calls=%fused_computation | loop fusion | flops 24576 | bytes 98304 | tf_op jit(solution)/shard_map/transpose | solution.py:409
  0.8 0.1 copy.13
  0.9 0.7 %reshape.8.weight_ref = f32[64,128]{1,0:T(8,128)} reshape(f32[512,16]{1,0:T(8,128)S(1)} %copy.13) | data formatting | bytes 65536 | tf_op jit(solution)/shard_map/reshape | solution.py:409
  1.7 1.5 %broadcast_in_dim.2.gain_ref = f32[512,128]{1,0:T(8,128)} broadcast(f32[512]{0:T(512)} %param.13), dimensions={0} | broadcast | bytes 264192 | tf_op jit(solution)/shard_map/broadcast_in_dim | solution.py:410
  3.2 0.9 %copy.12 = f32[512,16]{1,0:T(8,128)S(1)} copy(f32[512,16]{0,1:T(8,128)} %bitcast.3) | data formatting | bytes 65536 | tf_op jit(solution)/shard_map/transpose | solution.py:408
  4.1 0.7 %reshape.7.decay_ref = f32[64,128]{1,0:T(8,128)} reshape(f32[512,16]{1,0:T(8,128)S(1)} %copy.12) | data formatting | bytes 65536 | tf_op jit(solution)/shard_map/reshape | solution.py:408
  4.8 55.9 %shard_map.91 = f32[512,2048]{1,0:T(8,128)} custom-call(bf16[512,2048]{1,0:T(8,128)(2,1)} %sq_hbm.1, bf16[512,2048]{1,0:T(8,128)(2,1)} %sk_hbm.1, bf16[512,2048]{1,0:T(8,128)(2,1)} %sv_hbm.1, bf16[512,2048]{1,0:T(8,128)(2,1)} %lk_hbm.1, bf16[512,2048]{1,0:T(8,128)(2,1)} %lq_hbm.1, bf16[512,128]{1,0:T(8,128)(2,1)} %taps_ref.1, ...), custom_call_target="tpu_custom_call" | custom-call | tf_op jit(solution)/shard_map/pallas_call | solution.py:414
  60.7 4.7 %copy.15 = f32[512,2048]{1,0:T(8,128)} copy(f32[512,2048]{1,0:T(8,128)} %shard_map.91) | data formatting | bytes 8388608

commit v3 on v2

--- a/solution.py
+++ b/solution.py
@@ -21,11 +21,11 @@
     sv_hbm,
     lk_hbm,
     lq_hbm,
+    taps_hbm,
+    modes_hbm,
+    out_hbm,
     taps_ref,
-    gain_ref,
-    decay_ref,
-    weight_ref,
-    out_hbm,
+    modes_ref,
     sq,
     sk,
     sv,
@@ -46,6 +46,7 @@
     states,
     in_sem,
     edge_in_sem,
+    small_sem,
     out_sem,
     edge_sem,
     sum_send_sem,
@@ -68,12 +69,18 @@
             source.at[:, pl.ds(length - block, block)], target, edge_in_sem.at[which]
         )
 
+    def small_in(which, source, target):
+        return pltpu.make_async_copy(source, target, small_sem.at[which])
+
     def bring(which, source, target, chunk):
         rows = pl.ds(pl.multiple_of(chunk * chunk_rows, 16), chunk_rows)
         return pltpu.make_async_copy(source.at[rows], target.at[rows], in_sem.at[which, chunk])
 
     edge_in(0, sk_hbm, key_edge).start()
     edge_in(1, sv_hbm, value_edge).start()
+    small_in(0, taps_hbm, taps_ref).start()
+    small_in(1, modes_hbm, modes_ref).start()
+    decay_ref, weight_ref = modes_ref.at[0], modes_ref.at[1]
 
     def start_short(chunk, _):
         bring(0, sk_hbm, sk, chunk).start()
@@ -127,17 +134,29 @@
     lower_mask = jnp.where(col_id >= row_id, 1.0, 0.0).astype(BF16)
     upper_mask = jnp.where(col_id < row_id, 1.0, 0.0).astype(BF16)
     pick_row = lax.broadcasted_iota(jnp.int32, (16, block), 0) % SUB
-    row_masks = [jnp.where(pick_row == c, 1.0, 0.0).astype(BF16) for c in range(SUB)]
+    pair_masks = [jnp.where(pick_row // 2 == s, 1.0, 0.0).astype(BF16) for s in range(SUB // 2)]
     sub_id = lax.broadcasted_iota(jnp.int32, (SUB, block), 0)
     lane_id = lax.broadcasted_iota(jnp.int32, (SUB, block), 1)
     own_modes = (lane_id // (block // SUB)) == sub_id
 
-    def spread(stacked):
-        rows = stacked.shape[0]
-        tiled = stacked.reshape(rows // 16, 16, block)
+    odd_row = sub_id % 2 == 1
+
+    def spread(*stacks):
+        rows = stacks[0].shape[0]
         return jnp.concatenate(
-            [(tiled * row_masks[c][None]).reshape(rows, block) for c in range(SUB)], axis=1
-        )
+            [
+                (stacked.reshape(rows // 16, 16, block) * pair_masks[s][None]).reshape(rows, block)
+                for s in range(SUB // 2)
+                for stacked in stacks
+            ],
+            axis=1,
+        )
+
+    def beside(left, right):
+        return jnp.concatenate([left, right], axis=1)
+
+    def own_half(mixed, b):
+        return jnp.where(odd_row, mixed[over(b), block:], mixed[over(b), :block])
 
     def circulant(row):
         base = jnp.broadcast_to(row, (16, block))
@@ -161,24 +180,28 @@
         return slice(b * SUB, (b + 1) * SUB)
 
     step_at = col_id.astype(F32)
-    modes = block // SUB
 
     def make_params(step, _):
         for g in [step * 4 + i for i in range(4)]:
             decay = jnp.broadcast_to(decay_ref[pl.ds(g, 1), :], (block, block)).T
-            weight = jnp.broadcast_to(weight_ref[pl.ds(g, 1), :], (block, block)).T
-            tail = jnp.concatenate(parts(jnp.exp(-decay * (block - 1 - step_at))), axis=1)
-            kernel = weight * jnp.exp(-decay * step_at)
-            high, low = parts(weight * jnp.exp(-decay * (step_at + 1.0)))
-            band = []
-            for c in range(SUB):
-                row = jnp.sum(kernel[c * modes : (c + 1) * modes], axis=0, keepdims=True)
-                band.append(circulant(row) * lower_mask)
+            tail = beside(*parts(jnp.exp(-decay * (block - 1 - step_at))))
+            head = beside(*parts(jnp.exp(-decay * step_at)))
+            weight = jnp.where(own_modes, weight_ref[pl.ds(g, 1), :], 0.0)
+            sums_two = jnp.dot(
+                beside(*parts(weight)),
+                jnp.concatenate([head, head], axis=0),
+                preferred_element_type=F32,
+            )
+            kernel = sums_two[:, :block] + sums_two[:, block:]
+            band = [circulant(kernel[c : c + 1]) * lower_mask for c in range(SUB)]
             tails[g] = tail
-            heads[g] = jnp.concatenate([high, high, low], axis=0)
-            bands[g] = jnp.concatenate(band, axis=0)
-        return 0
-
+            heads[g] = head
+            for s in range(SUB // 2):
+                bands[g, s * block : (s + 1) * block, :] = beside(band[2 * s], band[2 * s + 1])
+        return 0
+
+    small_in(0, taps_hbm, taps_ref).wait()
+    small_in(1, modes_hbm, modes_ref).wait()
     lax.fori_loop(0, groups // 8, make_params, 0)
 
     squares[...] = jnp.zeros_like(squares)
@@ -194,26 +217,23 @@
         gates = []
         for half in range(2):
             own = slice(half * SUB, (half + 1) * SUB)
-            stacked = jnp.concatenate(
-                [edge[own]]
-                + [product[own, at(b)] for b in range(blocks)]
-                + [jnp.zeros((SUB, block), F32)],
-                axis=0,
-            ).astype(BF16)
+            tiles = [edge[own]] + [product[own, at(b)] for b in range(blocks)]
+            before = jnp.concatenate(tiles[:-1], axis=0).astype(BF16)
+            current = jnp.concatenate(tiles[1:], axis=0).astype(BF16)
+            turned = [circulant(taps[half * SUB + c : half * SUB + c + 1]) for c in range(SUB)]
             bands_now = []
-            for c in range(SUB):
-                turned = circulant(taps[half * SUB + c : half * SUB + c + 1])
-                bands_now.append(
-                    jnp.concatenate([turned * lower_mask, turned * upper_mask], axis=1)
-                )
+            for s in range(SUB // 2):
+                first, second = turned[2 * s], turned[2 * s + 1]
+                bands_now.append(beside(first * lower_mask, second * lower_mask))
+                bands_now.append(beside(first * upper_mask, second * upper_mask))
             mixed = jnp.dot(
-                spread(stacked),
+                spread(current, before),
                 jnp.concatenate(bands_now, axis=0),
                 preferred_element_type=F32,
             )
             gates.append(
                 [
-                    query[own, at(b)] * (mixed[over(b + 1), :block] + mixed[over(b), block:])
+                    query[own, at(b)] * own_half(mixed, b)
                     for b in range(blocks)
                 ]
             )
@@ -271,10 +291,9 @@
             own = slice(half * SUB, (half + 1) * SUB)
             g = pair * 2 + half
             place = pl.ds(pl.multiple_of(pair * 16 + half * SUB, SUB), SUB)
-            gain = gain_ref[place, :]
             stacked = jnp.concatenate(
                 [
-                    key[own, at(b)] * (gated[place, at(b)] * gain * squares[:, at(b)])
+                    key[own, at(b)] * (gated[place, at(b)] * squares[:, at(b)])
                     for b in range(blocks)
                 ],
                 axis=0,
@@ -324,7 +343,9 @@
         ]
         rows = pl.ds(pl.multiple_of(step * 4 * SUB, 4 * SUB), 4 * SUB)
         for b in range(blocks):
-            gated[rows, at(b)] = jnp.concatenate([inner[over(b)] for inner in inners], axis=0)
+            gated[rows, at(b)] = jnp.concatenate(
+                [own_half(inner, b) for inner in inners], axis=0
+            )
         return 0
 
     lax.fori_loop(0, groups // 4, inner_groups, 0)
@@ -361,12 +382,13 @@
             for b in range(blocks):
                 before.append(carry[g, over(b), :] + here)
                 here = here * fade
-            high, low = parts(jnp.concatenate(before, axis=0))
+            scale = weight_ref[pl.ds(g, 1), :] * jnp.exp(-decay_ref[pl.ds(g, 1), :])
             carried = jnp.dot(
-                jnp.concatenate([high, low, high], axis=1),
-                heads[g],
+                beside(*parts(jnp.concatenate(before, axis=0) * scale)),
+                jnp.concatenate([heads[g], heads[g]], axis=0),
                 preferred_element_type=F32,
             )
+            carried = carried[:, :block] + carried[:, block:]
             for b in range(blocks):
                 gated[place, at(b)] = query[own, at(b)] * (gated[place, at(b)] + carried[over(b)])
         return 0
@@ -404,19 +426,20 @@
     assert modes * SUB == block
     n_ctx, n_tp = lax.axis_size("ctx"), lax.axis_size("tp")
     chunks = min(8, channels // 16)
-    weights = residues * jnp.sqrt(-jnp.expm1(-2.0 * decay_rates))
-    decays = decay_rates.T.reshape(groups, block)
-    weights = weights.T.reshape(groups, block)
-    gains = jnp.broadcast_to(norm_gain[:, None], (channels, block))
+    weights = residues * jnp.sqrt(-jnp.expm1(-2.0 * decay_rates)) * norm_gain[None, :]
+    both = jnp.stack([decay_rates, weights]).transpose(0, 2, 1).reshape(2, groups, block)
     hbm = pl.BlockSpec(memory_space=pl.ANY)
-    vmem = pl.BlockSpec(memory_space=pltpu.VMEM)
     dma = pltpu.SemaphoreType.DMA
     return pl.pallas_call(
         functools.partial(fused, n_ctx, n_tp, channels * n_tp),
         out_shape=jax.ShapeDtypeStruct((channels, length), F32),
-        in_specs=[hbm] * 5 + [vmem] * 4,
+        in_specs=[hbm] * 7,
         out_specs=hbm,
-        scratch_shapes=[pltpu.VMEM((channels, length), BF16)] * 5
+        scratch_shapes=[
+            pltpu.VMEM((channels, block), BF16),
+            pltpu.VMEM((2, groups, block), F32),
+        ]
+        + [pltpu.VMEM((channels, length), BF16)] * 5
         + [pltpu.VMEM((channels, block), BF16)] * 4
         + [
             pltpu.VMEM((channels, length), F32),
@@ -424,11 +447,12 @@
             pltpu.VMEM((n_tp, 1, length), F32),
             pltpu.VMEM((groups, block, block), BF16),
             pltpu.VMEM((groups, block, 2 * block), BF16),
-            pltpu.VMEM((groups, 3 * block, block), BF16),
-            pltpu.VMEM((groups, SUB * block, block), BF16),
+            pltpu.VMEM((groups, block, 2 * block), BF16),
+            pltpu.VMEM((groups, SUB // 2 * block, 2 * block), BF16),
             pltpu.VMEM((groups, block, block), F32),
             pltpu.VMEM((n_ctx, groups, block), F32),
             dma((5, chunks)),
+            dma((2,)),
             dma((2,)),
             dma((chunks,)),
             dma((2,)),
@@ -447,9 +471,7 @@
         long_key,
         long_query,
         short_taps,
-        gains,
-        decays,
-        weights,
+        both,
     )
 
 

time: 65.7 us -> 51.8 us (0.79)
  Pallas kernels: 55.9 us -> 44.3 us
  local copies, waits for them, and re-layouts: 8.7 us -> 5.72 us
  other arithmetic: 0.8 us -> 1.57 us
    pallas_call x1, Pallas kernels: 55.9 us -> 44.3 us  [shards(): pl.pallas_call(functools.partial(fused, n_ctx, n_tp, channels * n_tp), ou...]
    broadcast_in_dim x1 -> x0, local copies, waits for them, and re-layouts: 1.52 us -> none  [shards(): gains = jnp.broadcast_to(norm_gain[:, None], (channels, block))]
    transpose x2 -> x1, local copies, waits for them, and re-layouts: 1 us -> 0.19 us  [shards(): jnp.stack([decay_rates, weights]).transpose(0, 2, 1)]
    another operation x0 -> x1, other arithmetic: none -> 0.81 us  [shards(): jnp.stack([decay_rates, weights]).transpose(0, 2, 1)]
    reshape x2 -> x1, local copies, waits for them, and re-layouts: 1.48 us -> 0.82 us  [shards(): jnp.stack([decay_rates, weights]).transpose(0, 2, 1)]
where the time goes in v3:
time: 51.8 us; the launch traced here: 51.6 us
  Pallas kernels  44.3 us (86%)
  local copies, waits for them, and re-layouts  5.72 us (11%)
  other arithmetic  1.57 us (3%)
    pallas_call x1, Pallas kernels, shards(): pl.pallas_call(functools.partial(fused, n_ctx, n_tp, channels * n_tp), ou...  44.3 us
    unnamed x1, local copies, waits for them, and re-layouts  4.7 us

profile of v3, /device:TPU:0, one launch (start us, length us, event | category | flops | bytes accessed | tf_op | source)
XLA Modules:
  0.0 51.6 jit_solution(14033947261500808099)
XLA Ops:
  0.0 0.8 %multiply_bitcast_fusion = f32[1,16,512]{2,1,0:T(8,128)S(1)} fusion(f32[16,512]{1,0:T(8,128)} %param.16, f32[16,512]{1,0:T(8,128)} %param.17, f32[512]{0:T(512)} %param.13), kind=kLoop, calls=%fused_computation.1 | loop fusion | flops 32768 | bytes 100352 | tf_op jit(solution)/shard_map/stack | solution.py:430
  0.8 0.8 %maximum_bitcast_fusion = f32[2,512,16]{1,2,0:T(8,128)S(1)} fusion(f32[1,16,512]{2,1,0:T(8,128)S(1)} %multiply_bitcast_fusion, f32[1,16,512]{2,1,0:T(8,128)} %bitcast.5), kind=kLoop, calls=%fused_computation | loop fusion | flops 16384 | bytes 131072 | tf_op jit(solution)/shard_map/transpose | solution.py:430
  1.6 0.2 copy.11
  1.8 0.8 %reshape.4.modes_hbm = f32[2,64,128]{2,1,0:T(8,128)} reshape(f32[2,512,16]{2,1,0:T(8,128)S(1)} %copy.11) | data formatting | bytes 131072 | tf_op jit(solution)/shard_map/reshape | solution.py:430
  2.6 44.3 %shard_map.91 = f32[512,2048]{1,0:T(8,128)} custom-call(bf16[512,2048]{1,0:T(8,128)(2,1)} %sq_hbm.1, bf16[512,2048]{1,0:T(8,128)(2,1)} %sk_hbm.1, bf16[512,2048]{1,0:T(8,128)(2,1)} %sv_hbm.1, bf16[512,2048]{1,0:T(8,128)(2,1)} %lk_hbm.1, bf16[512,2048]{1,0:T(8,128)(2,1)} %lq_hbm.1, bf16[512,128]{1,0:T(8,128)(2,1)} %taps_hbm.1, f32[2,64,128]{2,1,0:T(8,128)} %reshape.4.modes_hbm), custom_call_target="tpu_custom_call" | custom-call | tf_op jit(solution)/shard_map/pallas_call | solution.py:433
  46.9 4.7 %copy.13 = f32[512,2048]{1,0:T(8,128)} copy(f32[512,2048]{1,0:T(8,128)} %shard_map.91) | data formatting | bytes 8388608

commit v4 on v3

--- a/solution.py
+++ b/solution.py
@@ -43,6 +43,9 @@
     heads,
     bands,
     carry,
+    inner,
+    turn_in,
+    turn_out,
     states,
     in_sem,
     edge_in_sem,
@@ -61,6 +64,7 @@
     chunks = in_sem.shape[1]
     chunk_rows = channels // chunks
     pairs = chunk_rows // 16
+    per = min(2, pairs)
     my_ctx = lax.axis_index("ctx")
     my_tp = lax.axis_index("tp")
 
@@ -133,30 +137,15 @@
     col_id = lax.broadcasted_iota(jnp.int32, (block, block), 1)
     lower_mask = jnp.where(col_id >= row_id, 1.0, 0.0).astype(BF16)
     upper_mask = jnp.where(col_id < row_id, 1.0, 0.0).astype(BF16)
-    pick_row = lax.broadcasted_iota(jnp.int32, (16, block), 0) % SUB
-    pair_masks = [jnp.where(pick_row // 2 == s, 1.0, 0.0).astype(BF16) for s in range(SUB // 2)]
     sub_id = lax.broadcasted_iota(jnp.int32, (SUB, block), 0)
     lane_id = lax.broadcasted_iota(jnp.int32, (SUB, block), 1)
     own_modes = (lane_id // (block // SUB)) == sub_id
 
-    odd_row = sub_id % 2 == 1
-
-    def spread(*stacks):
-        rows = stacks[0].shape[0]
-        return jnp.concatenate(
-            [
-                (stacked.reshape(rows // 16, 16, block) * pair_masks[s][None]).reshape(rows, block)
-                for s in range(SUB // 2)
-                for stacked in stacks
-            ],
-            axis=1,
-        )
-
     def beside(left, right):
         return jnp.concatenate([left, right], axis=1)
 
-    def own_half(mixed, b):
-        return jnp.where(odd_row, mixed[over(b), block:], mixed[over(b), :block])
+    def channel_rows(first):
+        return pl.ds(first, blocks, stride=SUB)
 
     def circulant(row):
         base = jnp.broadcast_to(row, (16, block))
@@ -169,9 +158,11 @@
         return high, (value - high.astype(F32)).astype(BF16)
 
     def run_pairs(chunk, body):
-        lax.fori_loop(
-            0, pairs, lambda i, _: body(chunk * pairs + i, 0), 0, unroll=min(2, pairs)
-        )
+        def step(i, _):
+            body([chunk * pairs + i * per + k for k in range(per)])
+            return 0
+
+        lax.fori_loop(0, pairs // per, step, 0)
 
     def at(b):
         return slice(b * block, (b + 1) * block)
@@ -208,46 +199,57 @@
     edge_copy.wait()
     has_left = jnp.where(my_ctx > 0, 1.0, 0.0).astype(F32)
 
-    def short_pair(pair, _):
-        rows = pl.ds(pl.multiple_of(pair * 16, 16), 16)
-        product = sk[rows, :].astype(F32) * sv[rows, :].astype(F32)
-        query = sq[rows, :].astype(F32)
-        edge = edge_recv[rows, :].astype(F32) * has_left
-        taps = taps_ref[rows, :].astype(F32)
-        gates = []
-        for half in range(2):
-            own = slice(half * SUB, (half + 1) * SUB)
-            tiles = [edge[own]] + [product[own, at(b)] for b in range(blocks)]
-            before = jnp.concatenate(tiles[:-1], axis=0).astype(BF16)
-            current = jnp.concatenate(tiles[1:], axis=0).astype(BF16)
-            turned = [circulant(taps[half * SUB + c : half * SUB + c + 1]) for c in range(SUB)]
-            bands_now = []
-            for s in range(SUB // 2):
-                first, second = turned[2 * s], turned[2 * s + 1]
-                bands_now.append(beside(first * lower_mask, second * lower_mask))
-                bands_now.append(beside(first * upper_mask, second * upper_mask))
-            mixed = jnp.dot(
-                spread(current, before),
-                jnp.concatenate(bands_now, axis=0),
-                preferred_element_type=F32,
-            )
-            gates.append(
-                [
-                    query[own, at(b)] * own_half(mixed, b)
-                    for b in range(blocks)
-                ]
-            )
+    def short_pairs(todo):
+        places = [pl.ds(pl.multiple_of(pair * 16, 16), 16) for pair in todo]
+        for k, rows in enumerate(places):
+            product = sk[rows, :].astype(F32) * sv[rows, :].astype(F32)
+            edge = edge_recv[rows, :].astype(F32) * has_left
+            for half in range(2):
+                own = slice(half * SUB, (half + 1) * SUB)
+                turn_in[2 * k + half, over(0), :] = edge[own]
+                for b in range(blocks):
+                    turn_in[2 * k + half, over(b + 1), :] = product[own, at(b)]
+        for k, rows in enumerate(places):
+            taps = taps_ref[rows, :].astype(F32)
+            for half in range(2):
+                slot = 2 * k + half
+                for s in range(SUB // 2):
+                    windows, bands_now = [], []
+                    for c in (2 * s, 2 * s + 1):
+                        windows.append(
+                            beside(
+                                turn_in[slot, channel_rows(SUB + c), :].astype(BF16),
+                                turn_in[slot, channel_rows(c), :].astype(BF16),
+                            )
+                        )
+                        turned = circulant(taps[half * SUB + c : half * SUB + c + 1])
+                        bands_now.append(
+                            jnp.concatenate([turned * lower_mask, turned * upper_mask], axis=0)
+                        )
+                    mixed = jnp.dot(
+                        jnp.concatenate(windows, axis=0),
+                        beside(*bands_now),
+                        preferred_element_type=F32,
+                    )
+                    turn_out[slot, channel_rows(2 * s), :] = mixed[:blocks, :block]
+                    turn_out[slot, channel_rows(2 * s + 1), :] = mixed[blocks:, block:]
+        queries = [sq[rows, :].astype(F32) for rows in places]
         for b in range(blocks):
-            first, second = gates[0][b], gates[1][b]
-            gated[rows, at(b)] = jnp.concatenate([first, second], axis=0)
-            squares[:, at(b)] += first * first + second * second
-        return 0
+            square = squares[:, at(b)]
+            for k, rows in enumerate(places):
+                mix = jnp.concatenate(
+                    [turn_out[2 * k, over(b), :], turn_out[2 * k + 1, over(b), :]], axis=0
+                )
+                gate = queries[k][:, at(b)] * mix
+                gated[rows, at(b)] = gate
+                square = square + gate[:SUB] * gate[:SUB] + gate[SUB:] * gate[SUB:]
+            squares[:, at(b)] = square
 
     def short_chunk(chunk, _):
         bring(0, sk_hbm, sk, chunk).wait()
         bring(1, sv_hbm, sv, chunk).wait()
         bring(2, sq_hbm, sq, chunk).wait()
-        run_pairs(chunk, short_pair)
+        run_pairs(chunk, short_pairs)
         return 0
 
     lax.fori_loop(0, chunks, short_chunk, 0)
@@ -284,21 +286,25 @@
         total = total + sums[other]
     squares[...] = jnp.broadcast_to(lax.rsqrt(total / width + 1e-06), squares.shape)
 
-    def state_pair(pair, _):
+    def state_pair(pair, k):
         rows = pl.ds(pl.multiple_of(pair * 16, 16), 16)
         key = lk[rows, :].astype(F32)
         for half in range(2):
             own = slice(half * SUB, (half + 1) * SUB)
             g = pair * 2 + half
             place = pl.ds(pl.multiple_of(pair * 16 + half * SUB, SUB), SUB)
-            stacked = jnp.concatenate(
+            whole = jnp.concatenate(
                 [
                     key[own, at(b)] * (gated[place, at(b)] * squares[:, at(b)])
                     for b in range(blocks)
                 ],
                 axis=0,
+            )
+            stacked = whole.astype(BF16)
+            turn_out[2 * k + half] = whole
+            signal[g] = jnp.concatenate(
+                [turn_out[2 * k + half, channel_rows(c), :] for c in range(SUB)], axis=0
             ).astype(BF16)
-            signal[g] = stacked
             ends = lax.dot_general(
                 jnp.concatenate([stacked, stacked], axis=1),
                 tails[g],
@@ -311,11 +317,14 @@
                 carry[g, over(b), :] = state
                 state = fade * state + jnp.where(own_modes, ends[over(b)], 0.0)
             states[my_ctx, pl.ds(g, 1), :] = jnp.sum(state, axis=0, keepdims=True)
-        return 0
+
+    def state_pairs(todo):
+        for k, pair in enumerate(todo):
+            state_pair(pair, k)
 
     def state_chunk(chunk, _):
         bring(3, lk_hbm, lk, chunk).wait()
-        run_pairs(chunk, state_pair)
+        run_pairs(chunk, state_pairs)
         return 0
 
     lax.fori_loop(0, chunks, state_chunk, 0)
@@ -337,15 +346,23 @@
     lax.fori_loop(1, n_ctx, state_start, 0)
 
     def inner_groups(step, _):
-        inners = [
-            jnp.dot(spread(signal[step * 4 + i]), bands[step * 4 + i], preferred_element_type=F32)
-            for i in range(4)
-        ]
-        rows = pl.ds(pl.multiple_of(step * 4 * SUB, 4 * SUB), 4 * SUB)
-        for b in range(blocks):
-            gated[rows, at(b)] = jnp.concatenate(
-                [own_half(inner, b) for inner in inners], axis=0
-            )
+        for g in [step * 4 + i for i in range(4)]:
+            rows = signal[g]
+            for q in range(SUB // 4):
+                half = 2 * blocks
+                first = rows[2 * q * half : (2 * q + 1) * half]
+                second = rows[(2 * q + 1) * half : (2 * q + 2) * half]
+                empty = jnp.zeros_like(first)
+                mixed = jnp.dot(
+                    jnp.concatenate([beside(first, empty), beside(empty, second)], axis=0),
+                    bands[g, 2 * q * block : (2 * q + 2) * block, :],
+                    preferred_element_type=F32,
+                )
+                for c in range(4):
+                    side = slice((c % 2) * block, (c % 2 + 1) * block)
+                    inner[g, channel_rows(4 * q + c), :] = mixed[
+                        c * blocks : (c + 1) * blocks, side
+                    ]
         return 0
 
     lax.fori_loop(0, groups // 4, inner_groups, 0)
@@ -369,7 +386,7 @@
         rows = pl.ds(pl.multiple_of(chunk * chunk_rows, 16), chunk_rows)
         return pltpu.make_async_copy(gated.at[rows], out_hbm.at[rows], out_sem.at[chunk])
 
-    def last_pair(pair, _):
+    def last_pair(pair):
         rows = pl.ds(pl.multiple_of(pair * 16, 16), 16)
         query = lq[rows, :].astype(F32)
         for half in range(2):
@@ -390,12 +407,15 @@
             )
             carried = carried[:, :block] + carried[:, block:]
             for b in range(blocks):
-                gated[place, at(b)] = query[own, at(b)] * (gated[place, at(b)] + carried[over(b)])
-        return 0
+                gated[place, at(b)] = query[own, at(b)] * (inner[g, over(b), :] + carried[over(b)])
+
+    def last_pairs(todo):
+        for pair in todo:
+            last_pair(pair)
 
     def last_chunk(chunk, _):
         bring(4, lq_hbm, lq, chunk).wait()
-        run_pairs(chunk, last_pair)
+        run_pairs(chunk, last_pairs)
         out_copy(chunk).start()
         return 0
 
@@ -423,6 +443,7 @@
     block = short_taps.shape[1]
     modes = decay_rates.shape[0]
     groups = channels // SUB
+    rows = length // block * SUB
     assert modes * SUB == block
     n_ctx, n_tp = lax.axis_size("ctx"), lax.axis_size("tp")
     chunks = min(8, channels // 16)
@@ -445,11 +466,14 @@
             pltpu.VMEM((channels, length), F32),
             pltpu.VMEM((SUB, length), F32),
             pltpu.VMEM((n_tp, 1, length), F32),
-            pltpu.VMEM((groups, block, block), BF16),
+            pltpu.VMEM((groups, rows, block), BF16),
             pltpu.VMEM((groups, block, 2 * block), BF16),
             pltpu.VMEM((groups, block, 2 * block), BF16),
             pltpu.VMEM((groups, SUB // 2 * block, 2 * block), BF16),
-            pltpu.VMEM((groups, block, block), F32),
+            pltpu.VMEM((groups, rows, block), F32),
+            pltpu.VMEM((groups, rows, block), F32),
+            pltpu.VMEM((4, rows + SUB, block), F32),
+            pltpu.VMEM((4, rows, block), F32),
             pltpu.VMEM((n_ctx, groups, block), F32),
             dma((5, chunks)),
             dma((2,)),

time: 51.8 us -> 51 us (0.985)
  Pallas kernels: 44.3 us -> 43.4 us
    pallas_call x1, Pallas kernels: 44.3 us -> 43.4 us  [shards(): pl.pallas_call(functools.partial(fused, n_ctx, n_tp, channels * n_tp), ou...]
where the time goes in v4:
time: 51 us; the launch traced here: 50.7 us
  Pallas kernels  43.4 us (85%)
  local copies, waits for them, and re-layouts  5.72 us (11%)
  other arithmetic  1.57 us (3%)
    pallas_call x1, Pallas kernels, shards(): pl.pallas_call(functools.partial(fused, n_ctx, n_tp, channels * n_tp), ou...  43.4 us
    unnamed x1, local copies, waits for them, and re-layouts  4.7 us

profile of v4, /device:TPU:0, one launch (start us, length us, event | category | flops | bytes accessed | tf_op | source)
XLA Modules:
  0.0 50.7 jit_solution(392936737530110917)
XLA Ops:
  0.0 0.8 %multiply_bitcast_fusion = f32[1,16,512]{2,1,0:T(8,128)S(1)} fusion(f32[16,512]{1,0:T(8,128)} %param.16, f32[16,512]{1,0:T(8,128)} %param.17, f32[512]{0:T(512)} %param.13), kind=kLoop, calls=%fused_computation.1 | loop fusion | flops 32768 | bytes 100352 | tf_op jit(solution)/shard_map/stack | solution.py:451
  0.8 0.8 %maximum_bitcast_fusion = f32[2,512,16]{1,2,0:T(8,128)S(1)} fusion(f32[1,16,512]{2,1,0:T(8,128)S(1)} %multiply_bitcast_fusion, f32[1,16,512]{2,1,0:T(8,128)} %bitcast.5), kind=kLoop, calls=%fused_computation | loop fusion | flops 16384 | bytes 131072 | tf_op jit(solution)/shard_map/transpose | solution.py:451
  1.6 0.2 copy.11
  1.8 0.8 %reshape.4.modes_hbm = f32[2,64,128]{2,1,0:T(8,128)} reshape(f32[2,512,16]{2,1,0:T(8,128)S(1)} %copy.11) | data formatting | bytes 131072 | tf_op jit(solution)/shard_map/reshape | solution.py:451
  2.6 43.4 %shard_map.91 = f32[512,2048]{1,0:T(8,128)} custom-call(bf16[512,2048]{1,0:T(8,128)(2,1)} %sq_hbm.1, bf16[512,2048]{1,0:T(8,128)(2,1)} %sk_hbm.1, bf16[512,2048]{1,0:T(8,128)(2,1)} %sv_hbm.1, bf16[512,2048]{1,0:T(8,128)(2,1)} %lk_hbm.1, bf16[512,2048]{1,0:T(8,128)(2,1)} %lq_hbm.1, bf16[512,128]{1,0:T(8,128)(2,1)} %taps_hbm.1, f32[2,64,128]{2,1,0:T(8,128)} %reshape.4.modes_hbm), custom_call_target="tpu_custom_call" | custom-call | tf_op jit(solution)/shard_map/pallas_call | solution.py:454
  46.0 4.7 %copy.13 = f32[512,2048]{1,0:T(8,128)} copy(f32[512,2048]{1,0:T(8,128)} %shard_map.91) | data formatting | bytes 8388608

commit v5 on v4

--- a/solution.py
+++ b/solution.py
@@ -61,10 +61,11 @@
     block = taps_ref.shape[1]
     blocks = length // block
     groups = channels // SUB
+    many = min(8, groups // 2)
     chunks = in_sem.shape[1]
     chunk_rows = channels // chunks
     pairs = chunk_rows // 16
-    per = min(2, pairs)
+    per = min(4, pairs)
     my_ctx = lax.axis_index("ctx")
     my_tp = lax.axis_index("tp")
 
@@ -173,7 +174,7 @@
     step_at = col_id.astype(F32)
 
     def make_params(step, _):
-        for g in [step * 4 + i for i in range(4)]:
+        for g in [step * many + i for i in range(many)]:
             decay = jnp.broadcast_to(decay_ref[pl.ds(g, 1), :], (block, block)).T
             tail = beside(*parts(jnp.exp(-decay * (block - 1 - step_at))))
             head = beside(*parts(jnp.exp(-decay * step_at)))
@@ -193,7 +194,7 @@
 
     small_in(0, taps_hbm, taps_ref).wait()
     small_in(1, modes_hbm, modes_ref).wait()
-    lax.fori_loop(0, groups // 8, make_params, 0)
+    lax.fori_loop(0, groups // many // 2, make_params, 0)
 
     squares[...] = jnp.zeros_like(squares)
     edge_copy.wait()
@@ -272,7 +273,7 @@
 
     lax.fori_loop(1, n_tp, sum_start, 0)
 
-    lax.fori_loop(groups // 8, groups // 4, make_params, 0)
+    lax.fori_loop(groups // many // 2, groups // many, make_params, 0)
 
     def sum_wait(step, _):
         other = lax.rem(my_tp + step, n_tp)
@@ -346,7 +347,7 @@
     lax.fori_loop(1, n_ctx, state_start, 0)
 
     def inner_groups(step, _):
-        for g in [step * 4 + i for i in range(4)]:
+        for g in [step * many + i for i in range(many)]:
             rows = signal[g]
             for q in range(SUB // 4):
                 half = 2 * blocks
@@ -365,7 +366,7 @@
                     ]
         return 0
 
-    lax.fori_loop(0, groups // 4, inner_groups, 0)
+    lax.fori_loop(0, groups // many, inner_groups, 0)
 
     def state_wait(step, _):
         other = lax.rem(my_ctx + step, n_ctx)
@@ -472,8 +473,8 @@
             pltpu.VMEM((groups, SUB // 2 * block, 2 * block), BF16),
             pltpu.VMEM((groups, rows, block), F32),
             pltpu.VMEM((groups, rows, block), F32),
-            pltpu.VMEM((4, rows + SUB, block), F32),
-            pltpu.VMEM((4, rows, block), F32),
+            pltpu.VMEM((8, rows + SUB, block), F32),
+            pltpu.VMEM((8, rows, block), F32),
             pltpu.VMEM((n_ctx, groups, block), F32),
             dma((5, chunks)),
             dma((2,)),

time: 51 us -> 53.7 us (1.053)
  Pallas kernels: 43.4 us -> 46.1 us
    pallas_call x1, Pallas kernels: 43.4 us -> 46.1 us  [shards(): pl.pallas_call(functools.partial(fused, n_ctx, n_tp, channels * n_tp), ou...]
where the time goes in v5:
time: 53.7 us; the launch traced here: 53.4 us
  Pallas kernels  46.1 us (86%)
  local copies, waits for them, and re-layouts  5.72 us (11%)
  other arithmetic  1.57 us (3%)
    pallas_call x1, Pallas kernels, shards(): pl.pallas_call(functools.partial(fused, n_ctx, n_tp, channels * n_tp), ou...  46.1 us
    unnamed x1, local copies, waits for them, and re-layouts  4.7 us

profile of v5, /device:TPU:0, one launch (start us, length us, event | category | flops | bytes accessed | tf_op | source)
XLA Modules:
  0.0 53.4 jit_solution(4275114608892585628)
XLA Ops:
  0.0 0.8 %multiply_bitcast_fusion = f32[1,16,512]{2,1,0:T(8,128)S(1)} fusion(f32[16,512]{1,0:T(8,128)} %param.16, f32[16,512]{1,0:T(8,128)} %param.17, f32[512]{0:T(512)} %param.13), kind=kLoop, calls=%fused_computation.1 | loop fusion | flops 32768 | bytes 100352 | tf_op jit(solution)/shard_map/stack | solution.py:452
  0.8 0.8 %maximum_bitcast_fusion = f32[2,512,16]{1,2,0:T(8,128)S(1)} fusion(f32[1,16,512]{2,1,0:T(8,128)S(1)} %multiply_bitcast_fusion, f32[1,16,512]{2,1,0:T(8,128)} %bitcast.5), kind=kLoop, calls=%fused_computation | loop fusion | flops 16384 | bytes 131072 | tf_op jit(solution)/shard_map/transpose | solution.py:452
  1.6 0.2 copy.11
  1.8 0.8 %reshape.4.modes_hbm = f32[2,64,128]{2,1,0:T(8,128)} reshape(f32[2,512,16]{2,1,0:T(8,128)S(1)} %copy.11) | data formatting | bytes 131072 | tf_op jit(solution)/shard_map/reshape | solution.py:452
  2.6 46.1 %shard_map.91 = f32[512,2048]{1,0:T(8,128)} custom-call(bf16[512,2048]{1,0:T(8,128)(2,1)} %sq_hbm.1, bf16[512,2048]{1,0:T(8,128)(2,1)} %sk_hbm.1, bf16[512,2048]{1,0:T(8,128)(2,1)} %sv_hbm.1, bf16[512,2048]{1,0:T(8,128)(2,1)} %lk_hbm.1, bf16[512,2048]{1,0:T(8,128)(2,1)} %lq_hbm.1, bf16[512,128]{1,0:T(8,128)(2,1)} %taps_hbm.1, f32[2,64,128]{2,1,0:T(8,128)} %reshape.4.modes_hbm), custom_call_target="tpu_custom_call" | custom-call | tf_op jit(solution)/shard_map/pallas_call | solution.py:455
  48.7 4.7 %copy.13 = f32[512,2048]{1,0:T(8,128)} copy(f32[512,2048]{1,0:T(8,128)} %shard_map.91) | data formatting | bytes 8388608

commit v6 on v4

--- a/solution.py
+++ b/solution.py
@@ -20,17 +20,18 @@
     sk_hbm,
     sv_hbm,
     lk_hbm,
-    lq_hbm,
     taps_hbm,
     modes_hbm,
-    out_hbm,
+    inner_hbm,
+    carry_hbm,
+    heads_hbm,
+    entering_hbm,
     taps_ref,
     modes_ref,
     sq,
     sk,
     sv,
     lk,
-    lq,
     key_edge,
     value_edge,
     edge_send,
@@ -94,7 +95,6 @@
 
     def start_long(chunk, _):
         bring(3, lk_hbm, lk, chunk).start()
-        bring(4, lq_hbm, lq, chunk).start()
         return 0
 
     lax.fori_loop(0, chunks, start_short, 0)
@@ -197,6 +197,19 @@
 
     squares[...] = jnp.zeros_like(squares)
     edge_copy.wait()
+    def entering_out():
+        return pltpu.make_async_copy(states.at[0], entering_hbm, out_sem.at[0])
+
+    def heads_out():
+        return pltpu.make_async_copy(heads, heads_hbm, out_sem.at[1])
+
+    def carry_out():
+        return pltpu.make_async_copy(carry, carry_hbm, out_sem.at[2])
+
+    def inner_out(step):
+        some = pl.ds(step * 4, 4)
+        return pltpu.make_async_copy(inner.at[some], inner_hbm.at[some], out_sem.at[3 + step])
+
     has_left = jnp.where(my_ctx > 0, 1.0, 0.0).astype(F32)
 
     def short_pairs(todo):
@@ -273,6 +286,7 @@
     lax.fori_loop(1, n_tp, sum_start, 0)
 
     lax.fori_loop(groups // 8, groups // 4, make_params, 0)
+    heads_out().start()
 
     def sum_wait(step, _):
         other = lax.rem(my_tp + step, n_tp)
@@ -328,6 +342,7 @@
         return 0
 
     lax.fori_loop(0, chunks, state_chunk, 0)
+    carry_out().start()
 
     def state_copy(slot, other):
         return pltpu.make_async_remote_copy(
@@ -363,6 +378,7 @@
                     inner[g, channel_rows(4 * q + c), :] = mixed[
                         c * blocks : (c + 1) * blocks, side
                     ]
+        inner_out(step).start()
         return 0
 
     lax.fori_loop(0, groups // 4, inner_groups, 0)
@@ -381,51 +397,56 @@
         further = device_fade * entering + states[other]
         entering = jnp.where(other < my_ctx, further, entering)
     states[0] = entering
-
-    def out_copy(chunk):
-        rows = pl.ds(pl.multiple_of(chunk * chunk_rows, 16), chunk_rows)
-        return pltpu.make_async_copy(gated.at[rows], out_hbm.at[rows], out_sem.at[chunk])
-
-    def last_pair(pair):
+    entering_out().start()
+    entering_out().wait()
+    heads_out().wait()
+    carry_out().wait()
+
+    def inner_wait(step, _):
+        inner_out(step).wait()
+        return 0
+
+    lax.fori_loop(0, groups // 4, inner_wait, 0)
+
+
+def finish(query_ref, inner_ref, carry_ref, heads_ref, entering_ref, modes_ref, out_ref):
+    here_groups, block = entering_ref.shape
+    blocks = out_ref.shape[1] // block
+    sub_id = lax.broadcasted_iota(jnp.int32, (SUB, block), 0)
+    lane_id = lax.broadcasted_iota(jnp.int32, (SUB, block), 1)
+    own_modes = (lane_id // (block // SUB)) == sub_id
+
+    def parts(value):
+        high = value.astype(BF16)
+        return high, (value - high.astype(F32)).astype(BF16)
+
+    def pair_step(pair, _):
         rows = pl.ds(pl.multiple_of(pair * 16, 16), 16)
-        query = lq[rows, :].astype(F32)
+        query = query_ref[rows, :].astype(F32)
+        mixes = []
         for half in range(2):
-            own = slice(half * SUB, (half + 1) * SUB)
             g = pair * 2 + half
-            place = pl.ds(pl.multiple_of(pair * 16 + half * SUB, SUB), SUB)
-            fade = jnp.exp(-decay_ref[pl.ds(g, 1), :] * block)
-            here = jnp.where(own_modes, states[0, pl.ds(g, 1), :], 0.0)
+            decay = modes_ref[0, pl.ds(g, 1), :]
+            fade = jnp.exp(-decay * block)
+            here = jnp.where(own_modes, entering_ref[pl.ds(g, 1), :], 0.0)
             before = []
             for b in range(blocks):
-                before.append(carry[g, over(b), :] + here)
+                before.append(carry_ref[g, b * SUB : (b + 1) * SUB, :] + here)
                 here = here * fade
-            scale = weight_ref[pl.ds(g, 1), :] * jnp.exp(-decay_ref[pl.ds(g, 1), :])
+            scale = modes_ref[1, pl.ds(g, 1), :] * jnp.exp(-decay)
+            head = heads_ref[g]
             carried = jnp.dot(
-                beside(*parts(jnp.concatenate(before, axis=0) * scale)),
-                jnp.concatenate([heads[g], heads[g]], axis=0),
+                jnp.concatenate(parts(jnp.concatenate(before, axis=0) * scale), axis=1),
+                jnp.concatenate([head, head], axis=0),
                 preferred_element_type=F32,
             )
-            carried = carried[:, :block] + carried[:, block:]
-            for b in range(blocks):
-                gated[place, at(b)] = query[own, at(b)] * (inner[g, over(b), :] + carried[over(b)])
-
-    def last_pairs(todo):
-        for pair in todo:
-            last_pair(pair)
-
-    def last_chunk(chunk, _):
-        bring(4, lq_hbm, lq, chunk).wait()
-        run_pairs(chunk, last_pairs)
-        out_copy(chunk).start()
-        return 0
-
-    lax.fori_loop(0, chunks, last_chunk, 0)
-
-    def out_wait(chunk, _):
-        out_copy(chunk).wait()
-        return 0
-
-    lax.fori_loop(0, chunks, out_wait, 0)
+            mixes.append(inner_ref[g] + carried[:, :block] + carried[:, block:])
+        for b in range(blocks):
+            own, at = slice(b * SUB, (b + 1) * SUB), slice(b * block, (b + 1) * block)
+            out_ref[rows, at] = query[:, at] * jnp.concatenate([mix[own] for mix in mixes], axis=0)
+        return 0
+
+    lax.fori_loop(0, here_groups // 2, pair_step, 0, unroll=2)
 
 
 def shards(
@@ -451,16 +472,21 @@
     both = jnp.stack([decay_rates, weights]).transpose(0, 2, 1).reshape(2, groups, block)
     hbm = pl.BlockSpec(memory_space=pl.ANY)
     dma = pltpu.SemaphoreType.DMA
-    return pl.pallas_call(
+    inner, carry, heads, entering = pl.pallas_call(
         functools.partial(fused, n_ctx, n_tp, channels * n_tp),
-        out_shape=jax.ShapeDtypeStruct((channels, length), F32),
-        in_specs=[hbm] * 7,
-        out_specs=hbm,
+        out_shape=[
+            jax.ShapeDtypeStruct((groups, rows, block), F32),
+            jax.ShapeDtypeStruct((groups, rows, block), F32),
+            jax.ShapeDtypeStruct((groups, block, 2 * block), BF16),
+            jax.ShapeDtypeStruct((groups, block), F32),
+        ],
+        in_specs=[hbm] * 6,
+        out_specs=[hbm] * 4,
         scratch_shapes=[
             pltpu.VMEM((channels, block), BF16),
             pltpu.VMEM((2, groups, block), F32),
         ]
-        + [pltpu.VMEM((channels, length), BF16)] * 5
+        + [pltpu.VMEM((channels, length), BF16)] * 4
         + [pltpu.VMEM((channels, block), BF16)] * 4
         + [
             pltpu.VMEM((channels, length), F32),
@@ -475,10 +501,10 @@
             pltpu.VMEM((4, rows + SUB, block), F32),
             pltpu.VMEM((4, rows, block), F32),
             pltpu.VMEM((n_ctx, groups, block), F32),
-            dma((5, chunks)),
+            dma((4, chunks)),
             dma((2,)),
             dma((2,)),
-            dma((chunks,)),
+            dma((3 + groups // 4,)),
             dma((2,)),
             dma((n_tp,)),
             dma((n_tp,)),
@@ -493,10 +519,31 @@
         short_key,
         short_value,
         long_key,
-        long_query,
         short_taps,
         both,
     )
+    own = min(8, groups)
+
+    def block_of(array):
+        rest = array.shape[1:]
+        return pl.BlockSpec((own,) + rest, lambda i: (i,) + (0,) * len(rest))
+
+    wide = pl.BlockSpec((own * SUB, length), lambda i: (i, 0))
+    return pl.pallas_call(
+        finish,
+        grid=(groups // own,),
+        out_shape=jax.ShapeDtypeStruct((channels, length), F32),
+        in_specs=[
+            wide,
+            block_of(inner),
+            block_of(carry),
+            block_of(heads),
+            block_of(entering),
+            pl.BlockSpec((2, own, block), lambda i: (0, i, 0)),
+        ],
+        out_specs=wide,
+        compiler_params=pltpu.CompilerParams(vmem_limit_bytes=32 * 1024 * 1024),
+    )(long_query, inner, carry, heads, entering, both)
 
 
 def solution(mesh):

time: 51 us -> 55.4 us (1.086)
  local copies, waits for them, and re-layouts: 5.72 us -> 8.34 us
  Pallas kernels: 43.4 us -> 45 us
    pallas_call x0 -> x1, Pallas kernels: none -> 5.63 us  [shards(): pl.pallas_call(finish, grid=(groups // own,), out_shape=jax.ShapeDtypeStr...]
    pallas_call x1, Pallas kernels: 43.4 us -> 39.4 us  [shards(): pl.pallas_call(functools.partial(fused, n_ctx, n_tp, channels * n_tp), ou...]
    unnamed x1 -> x12, local copies, waits for them, and re-layouts: 4.7 us -> 7.32 us
where the time goes in v6:
time: 55.4 us; the launch traced here: 55 us
  Pallas kernels  45 us (81%)
  local copies, waits for them, and re-layouts  8.34 us (15%)
  other arithmetic  1.57 us (3%)
    pallas_call x1, Pallas kernels, shards(): pl.pallas_call(functools.partial(fused, n_ctx, n_tp, channels * n_tp), ou...  39.4 us
    unnamed x12, local copies, waits for them, and re-layouts  7.32 us
    pallas_call x1, Pallas kernels, shards(): pl.pallas_call(finish, grid=(groups // own,), out_shape=jax.ShapeDtypeStr...  5.63 us

profile of v6, /device:TPU:0, one launch (start us, length us, event | category | flops | bytes accessed | tf_op | source)
XLA Modules:
  0.0 55.0 jit_solution(3794038396888997474)
XLA Ops:
  0.0 0.8 %multiply_bitcast_fusion = f32[1,16,512]{2,1,0:T(8,128)S(1)} fusion(f32[16,512]{1,0:T(8,128)} %param.16, f32[16,512]{1,0:T(8,128)} %param.17, f32[512]{0:T(512)} %param.13), kind=kLoop, calls=%fused_computation.1 | loop fusion | flops 32768 | bytes 100352 | tf_op jit(solution)/shard_map/stack | solution.py:472
  0.8 0.8 %maximum_bitcast_fusion = f32[2,512,16]{1,2,0:T(8,128)S(1)} fusion(f32[1,16,512]{2,1,0:T(8,128)S(1)} %multiply_bitcast_fusion, f32[1,16,512]{2,1,0:T(8,128)} %bitcast.5), kind=kLoop, calls=%fused_computation | loop fusion | flops 16384 | bytes 131072 | tf_op jit(solution)/shard_map/transpose | solution.py:472
  1.6 0.2 copy.11
  1.8 0.8 %reshape.4.modes_hbm.modes_ref = f32[2,64,128]{2,1,0:T(8,128)} reshape(f32[2,512,16]{2,1,0:T(8,128)S(1)} %copy.11) | data formatting | bytes 131072 | tf_op jit(solution)/shard_map/reshape | solution.py:472
  2.6 0.0 copy-start.3
  2.6 0.0 copy-start.4
  2.6 39.4 %shard_map.91 = (f32[64,128,128]{2,1,0:T(8,128)}, f32[64,128,128]{2,1,0:T(8,128)}, bf16[64,128,256]{2,1,0:T(8,128)(2,1)}, f32[64,128]{1,0:T(8,128)}) custom-call(bf16[512,2048]{1,0:T(8,128)(2,1)} %sq_hbm.1, bf16[512,2048]{1,0:T(8,128)(2,1)} %sk_hbm.1, bf16[512,2048]{1,0:T(8,128)(2,1)} %sv_hbm.1, bf16[512,2048]{1,0:T(8,128)(2,1)} %lk_hbm.1, ...), custom_call_target="tpu_custom_call" | custom-call | tf_op jit(solution)/shard_map/pallas_call | solution.py:475
  42.0 0.0 copy-done.3
  42.0 0.0 copy-done.4
  42.1 0.0 copy-start
  42.1 2.2 %copy-done = f32[64,128,128]{2,1,0:T(8,128)S(1)} copy-done((f32[64,128,128]{2,1,0:T(8,128)S(1)}, f32[64,128,128]{2,1,0:T(8,128)}, u32[]{:S(2)}) %copy-start) | copy-done | bytes 4194328
  44.2 0.0 copy-start.1
  44.2 2.2 %copy-done.1 = f32[64,128,128]{2,1,0:T(8,128)S(1)} copy-done((f32[64,128,128]{2,1,0:T(8,128)S(1)}, f32[64,128,128]{2,1,0:T(8,128)}, u32[]{:S(2)}) %copy-start.1) | copy-done | bytes 4194328
  46.4 0.0 copy-start.2
  46.4 2.2 %copy-done.2 = bf16[64,128,256]{2,1,0:T(8,128)(2,1)S(1)} copy-done((bf16[64,128,256]{2,1,0:T(8,128)(2,1)S(1)}, bf16[64,128,256]{2,1,0:T(8,128)(2,1)}, u32[]{:S(2)}) %copy-start.2) | copy-done | bytes 4194328
  48.6 0.0 copy-start.5
  48.6 0.8 %copy-done.5 = f32[64,128]{1,0:T(8,128)S(1)} copy-done((f32[64,128]{1,0:T(8,128)S(1)}, f32[64,128]{1,0:T(8,128)}, u32[]{:S(2)}) %copy-start.5) | copy-done | bytes 32792
  49.4 5.6 %shard_map.92 = f32[512,2048]{1,0:T(8,128)} custom-call(bf16[512,2048]{1,0:T(8,128)(2,1)S(1)} %copy-done.3, f32[64,128,128]{2,1,0:T(8,128)S(1)} %copy-done, f32[64,128,128]{2,1,0:T(8,128)S(1)} %copy-done.1, bf16[64,128,256]{2,1,0:T(8,128)(2,1)S(1)} %copy-done.2, f32[64,128]{1,0:T(8,128)S(1)} %copy-done.5, f32[2,64,128]{2,1,0:T(8,128)S(1)} %copy-done.4), custom_call_target="tpu_custom_call" | custom-call | tf_op jit(solution)/shard_map/pallas_call | solution.py:532
Async XLA Ops:
  2.6 39.4 %copy-start.3 = (bf16[512,2048]{1,0:T(8,128)(2,1)S(1)}, bf16[512,2048]{1,0:T(8,128)(2,1)}, u32[]{:S(2)}) copy-start(bf16[512,2048]{1,0:T(8,128)(2,1)} %query_ref.1) | copy-start | bytes 6291460
  2.6 39.4 %copy-start.4 = (f32[2,64,128]{2,1,0:T(8,128)S(1)}, f32[2,64,128]{2,1,0:T(8,128)}, u32[]{:S(2)}) copy-start(f32[2,64,128]{2,1,0:T(8,128)} %reshape.4.modes_hbm.modes_ref) | copy-start | bytes 196612
  42.1 2.2 %copy-start = (f32[64,128,128]{2,1,0:T(8,128)S(1)}, f32[64,128,128]{2,1,0:T(8,128)}, u32[]{:S(2)}) copy-start(f32[64,128,128]{2,1,0:T(8,128)} %get-tuple-element.9.inner_ref) | copy-start | bytes 12582916
  44.2 2.2 %copy-start.1 = (f32[64,128,128]{2,1,0:T(8,128)S(1)}, f32[64,128,128]{2,1,0:T(8,128)}, u32[]{:S(2)}) copy-start(f32[64,128,128]{2,1,0:T(8,128)} %get-tuple-element.10.carry_ref) | copy-start | bytes 12582916
  46.4 2.2 %copy-start.2 = (bf16[64,128,256]{2,1,0:T(8,128)(2,1)S(1)}, bf16[64,128,256]{2,1,0:T(8,128)(2,1)}, u32[]{:S(2)}) copy-start(bf16[64,128,256]{2,1,0:T(8,128)(2,1)} %get-tuple-element.11.heads_ref) | copy-start | bytes 12582916
  48.6 0.8 %copy-start.5 = (f32[64,128]{1,0:T(8,128)S(1)}, f32[64,128]{1,0:T(8,128)}, u32[]{:S(2)}) copy-start(f32[64,128]{1,0:T(8,128)} %get-tuple-element.12.entering_ref) | copy-start | bytes 98308

commit v7 on v6

--- a/solution.py
+++ b/solution.py
@@ -542,7 +542,7 @@
             pl.BlockSpec((2, own, block), lambda i: (0, i, 0)),
         ],
         out_specs=wide,
-        compiler_params=pltpu.CompilerParams(vmem_limit_bytes=32 * 1024 * 1024),
+        compiler_params=pltpu.CompilerParams(vmem_limit_bytes=60 * 1024 * 1024),
     )(long_query, inner, carry, heads, entering, both)
 
 

time: 55.4 us -> 52.8 us (0.953)
  local copies, waits for them, and re-layouts: 8.34 us -> 1.03 us
  Pallas kernels: 45 us -> 49.8 us
    unnamed x12 -> x0, local copies, waits for them, and re-layouts: 7.32 us -> none
    pallas_call x1, Pallas kernels: 5.63 us -> 10.4 us  [shards(): pl.pallas_call(finish, grid=(groups // own,), out_shape=jax.ShapeDtypeStr...]
where the time goes in v7:
time: 52.8 us; the launch traced here: 52.4 us
  Pallas kernels  49.8 us (94%)
  other arithmetic  1.57 us (3%)
  local copies, waits for them, and re-layouts  1.03 us (2%)
    pallas_call x1, Pallas kernels, shards(): pl.pallas_call(functools.partial(fused, n_ctx, n_tp, channels * n_tp), ou...  39.4 us
    pallas_call x1, Pallas kernels, shards(): pl.pallas_call(finish, grid=(groups // own,), out_shape=jax.ShapeDtypeStr...  10.4 us

profile of v7, /device:TPU:0, one launch (start us, length us, event | category | flops | bytes accessed | tf_op | source)
XLA Modules:
  0.0 52.4 jit_solution(2198717059217386648)
XLA Ops:
  0.0 0.8 %multiply_bitcast_fusion = f32[1,16,512]{2,1,0:T(8,128)S(1)} fusion(f32[16,512]{1,0:T(8,128)} %param.16, f32[16,512]{1,0:T(8,128)} %param.17, f32[512]{0:T(512)} %param.13), kind=kLoop, calls=%fused_computation.1 | loop fusion | flops 32768 | bytes 100352 | tf_op jit(solution)/shard_map/stack | solution.py:472
  0.8 0.8 %maximum_bitcast_fusion = f32[2,512,16]{1,2,0:T(8,128)S(1)} fusion(f32[1,16,512]{2,1,0:T(8,128)S(1)} %multiply_bitcast_fusion, f32[1,16,512]{2,1,0:T(8,128)} %bitcast.5), kind=kLoop, calls=%fused_computation | loop fusion | flops 16384 | bytes 131072 | tf_op jit(solution)/shard_map/transpose | solution.py:472
  1.6 0.2 copy.11
  1.8 0.8 %reshape.4.modes_hbm.modes_ref = f32[2,64,128]{2,1,0:T(8,128)} reshape(f32[2,512,16]{2,1,0:T(8,128)S(1)} %copy.11) | data formatting | bytes 131072 | tf_op jit(solution)/shard_map/reshape | solution.py:472
  2.6 39.4 %shard_map.91 = (f32[64,128,128]{2,1,0:T(8,128)}, f32[64,128,128]{2,1,0:T(8,128)}, bf16[64,128,256]{2,1,0:T(8,128)(2,1)}, f32[64,128]{1,0:T(8,128)}) custom-call(bf16[512,2048]{1,0:T(8,128)(2,1)} %sq_hbm.1, bf16[512,2048]{1,0:T(8,128)(2,1)} %sk_hbm.1, bf16[512,2048]{1,0:T(8,128)(2,1)} %sv_hbm.1, bf16[512,2048]{1,0:T(8,128)(2,1)} %lk_hbm.1, ...), custom_call_target="tpu_custom_call" | custom-call | tf_op jit(solution)/shard_map/pallas_call | solution.py:475
  42.0 10.4 %shard_map.92 = f32[512,2048]{1,0:T(8,128)} custom-call(bf16[512,2048]{1,0:T(8,128)(2,1)} %query_ref.1, f32[64,128,128]{2,1,0:T(8,128)} %get-tuple-element.9.inner_ref, f32[64,128,128]{2,1,0:T(8,128)} %get-tuple-element.10.carry_ref, bf16[64,128,256]{2,1,0:T(8,128)(2,1)} %get-tuple-element.11.heads_ref, f32[64,128]{1,0:T(8,128)} %get-tuple-element.12.entering_ref, ...), custom_call_target="tpu_custom_call" | custom-call | tf_op jit(solution)/shard_map/pallas_call | solution.py:532
